TPU v7x, 512 devices: a whole 4x8x8 slice. The times are simulated.
512 devices in a mesh: dp: 16 (over x_hi, y), tile: 32 (over z, x_lo, core).
Axes of the slice: x: 4 (x_hi: 2, x_lo: 2; x = x_hi * 2 + x_lo), y: 8, z: 8, core: 2. Of those that a mesh axis runs over, the one named last changes fastest.
Arguments:
- records: bfloat16 [16, 32768, 256], P('dp', 'tile'), may hold values from -6 to 6
- obs_tile: int32 [16, 32768, 1], P('dp', 'tile'), may hold values from 0 to 31; in each aligned block of 1024 rows (0 to 1023, 1024 to 2047, ..., all dimensions but the last counted through in order) at most 128 rows name the same one
- obs_cell: int32 [16, 32768], P('dp', 'tile'), may hold values from 0 to 1023
- conv_weight: bfloat16 [2304, 384], P('dp'), may hold values from -0.125 to 0.125
- cotangent: bfloat16 [16, 128, 256, 384], P('dp', 'tile'), may hold values from -0.032958984 to 0.032958984
Outputs:
- weight_grad: float32 [2304, 384], P('dp')
Inputs may be any that keep to these rules, and one draw needn't show every extreme that they name: `obs_tile`: among the 1024 records held by one device, no tile is named by more than 128 of them, a bound that some block reaches.
All inputs are finite; a program needn't handle non-finite values.
Results may differ from a plain program's by a relative error of at most 0.0035.
Values may be sent and summed in bfloat16 or wider, within the bound.
A program may use at most 64 MiB of HBM per device.

v0:
```python
import jax
import jax.numpy as jnp
from jax import lax
from jax.sharding import PartitionSpec as P


def extended(cells, sides, width):
    for axis, dim in sides:
        count = lax.axis_size(axis)
        ends = count - 1
        head = lax.slice_in_dim(cells, 0, width, axis=dim)
        tail = lax.slice_in_dim(cells, cells.shape[dim] - width, cells.shape[dim], axis=dim)
        cells = jnp.concatenate(
            [
                lax.ppermute(tail, axis, [(i, (i + 1) % count) for i in range(ends)]),
                cells,
                lax.ppermute(head, axis, [((i + 1) % count, i) for i in range(ends)]),
            ],
            axis=dim,
        )
    return cells


def local(records, obs_tile, obs_cell, conv_weight, cotangent):
    ntiles = lax.axis_size("tile")
    obs_count = records.shape[1]
    dobs = records.shape[2]
    capacity = obs_count // 8
    lat_rows = cotangent.shape[1]
    lon_cells = cotangent.shape[2]
    channels = cotangent.shape[3]
    cells_here = lat_rows * lon_cells
    dest = obs_tile[0, :, 0]
    marks = (dest[:, None] == jnp.arange(ntiles, dtype=jnp.int32)[None, :]).astype(jnp.int32)
    before = jnp.cumsum(marks, axis=0) - marks
    position = jnp.sum(before * marks, axis=1)
    slot = dest * capacity + position
    send_feat = jnp.zeros((ntiles * capacity, dobs), jnp.bfloat16).at[slot].set(records[0])
    send_cell = jnp.full((ntiles * capacity,), -1, jnp.int32).at[slot].set(obs_cell[0])
    recv_feat, recv_cell = (
        lax.all_to_all(
            send_feat.reshape(ntiles, capacity, dobs),
            "tile",
            split_axis=0,
            concat_axis=0,
            tiled=True,
        ),
        lax.all_to_all(
            send_cell.reshape(ntiles, capacity), "tile", split_axis=0, concat_axis=0, tiled=True
        ),
    )
    recv_feat = recv_feat.reshape(ntiles * capacity, dobs)
    recv_cell = recv_cell.reshape(ntiles * capacity)
    block = min(512, cells_here)
    while cells_here % block != 0:
        block = block // 2
    cell_ids = jnp.arange(cells_here, dtype=jnp.int32).reshape(cells_here // block, block)

    def set_conv(ids):
        equal = recv_cell[None, :] == ids[:, None]
        dens = jnp.sum(equal, axis=1).astype(jnp.float32)
        summed = jnp.dot(equal.astype(jnp.bfloat16), recv_feat, preferred_element_type=jnp.float32)
        return (summed / (dens[:, None] + 1.0)).astype(jnp.bfloat16)

    grid = lax.map(set_conv, cell_ids).reshape(lat_rows, lon_cells, dobs)
    rimmed = extended(grid, (("tile", 0),), 1)
    wrapped = jnp.concatenate([rimmed[:, -1:], rimmed, rimmed[:, :1]], axis=1)
    patches = []
    for lat_off in range(3):
        for lon_off in range(3):
            patches.append(wrapped[lat_off : lat_off + lat_rows, lon_off : lon_off + lon_cells])
    columns = jnp.concatenate(patches, axis=-1).reshape(cells_here, 9 * dobs)
    pre = jnp.dot(
        columns,
        lax.all_gather(conv_weight, "dp", axis=0, tiled=True),
        preferred_element_type=jnp.float32,
    )
    _, back = jax.vjp(jax.nn.gelu, pre)
    gpre = back(cotangent[0].reshape(cells_here, channels).astype(jnp.float32))[0].astype(
        jnp.bfloat16
    )
    full_grad = lax.dot_general(
        columns, gpre, (((0,), (0,)), ((), ())), preferred_element_type=jnp.float32
    )
    summed = lax.psum(full_grad, "tile")
    result = lax.psum_scatter(summed, "dp", scatter_dimension=0, tiled=True)
    return result


def solution(mesh):
    placed = (
        P("dp", "tile", None),
        P("dp", "tile", None),
        P("dp", "tile"),
        P("dp", None),
        P("dp", "tile", None, None),
    )
    return jax.shard_map(
        local, mesh=mesh, in_specs=placed, out_specs=P("dp", None), check_vma=False
    )
```

profile of v0, /device:TPU:1, one launch (start us, length us, event | category | flops | bytes accessed | tf_op | source)
XLA Modules:
  0.0 602.3 jit_solution(12751534131050040895)
XLA Ops:
  7.3 9.0 %reduce-window.6 = s32[32,8,128]{2,1,0:T(8,128)S(1)} reduce-window(s32[32,8,128]{2,1,0:T(8,128)S(1)} %fusion.43, s32[]{:T(128)} %copy.31), window={size=1x1x128 pad=0_0x0_0x127_0}, to_apply=%region_0.0 | reduce-window | flops 4161536 | bytes 262148 | tf_op jit(solution)/shard_map/reduce-window
  18.2 5.1 scatter_custom_fusion
  23.3 12.9 %all-to-all-start = ((s32[32,1,128]{2,1,0:T(1,128)}), s32[32,1,128]{2,1,0:T(1,128)S(1)}, u32[]{:S(2)}, u32[]{:S(2)}) async-start(s32[32,1,128]{2,1,0:T(1,128)} %bitcast.11), calls=%async_computation | async-start | bytes 32768 | tf_op jit(solution)/shard_map/all_to_all | solution.py:48
  36.2 6.6 %scatter_custom_fusion.1 = bf16[4096,256]{1,0:T(8,128)(2,1)} fusion(s32[1024]{0:T(1024)S(1)} %bitcast.96, bf16[]{:T(256)} %constant.12.clone.1, bf16[1,1024,256]{2,1,0:T(8,128)(2,1)S(1)} %copy-done), kind=kCustom, calls=%fused_computation.28 | custom fusion | bytes 2621442 | tf_op jit(solution)/shard_map/scatter | solution.py:38
  42.8 1.1 all-to-all-done
  43.9 7.1 %all-to-all-start.1 = ((bf16[32,128,256]{2,1,0:T(8,128)(2,1)}), bf16[32,128,256]{2,1,0:T(8,128)(2,1)S(1)}, u32[]{:S(2)}, u32[]{:S(2)}) async-start(bf16[32,128,256]{2,1,0:T(8,128)(2,1)} %bitcast.14), calls=%async_computation.1 | async-start | bytes 4194304 | tf_op jit(solution)/shard_map/all_to_all | solution.py:41
  51.9 49.3 %all-to-all-done.1 = bf16[32,128,256]{2,1,0:T(8,128)(2,1)S(1)} async-done(((bf16[32,128,256]{2,1,0:T(8,128)(2,1)}), bf16[32,128,256]{2,1,0:T(8,128)(2,1)S(1)}, u32[]{:S(2)}, u32[]{:S(2)}) %all-to-all-start.1) | async-done | bytes 2097184 | tf_op jit(solution)/shard_map/all_to_all | solution.py:41
  101.2 4.7 while.10
  101.2 1.0 fusion.74
  102.2 1.3 fusion.75
  103.5 1.0 fusion.74
  104.6 1.3 fusion.75
  105.9 3.7 collective-permute-start
  109.6 2.1 collective-permute-start.1
  112.3 6.8 %collective-permute-done.1 = bf16[1,256,256]{2,1,0:T(8,128)(2,1)S(1)} collective-permute-done((bf16[1,256,256]{2,1,0:T(8,128)(2,1)S(1)}, bf16[1,256,256]{2,1,0:T(8,128)(2,1)S(1)}, u32[]{:S(2)}, u32[]{:S(2)}) %collective-permute-start.1) | collective-permute-done | bytes 131104 | tf_op jit(solution)/shard_map/ppermute | solution.py:17
  121.5 0.9 constant_dynamic-update-slice_fusion.6
  122.3 0.9 constant_dynamic-update-slice_fusion.5
  123.2 0.9 constant_dynamic-update-slice_fusion.4
  124.1 0.9 constant_dynamic-update-slice_fusion.3
  127.6 15.5 %all-gather.2.cloned.1.call-done = bf16[2304,384]{1,0:T(8,128)(2,1)} async-done(((bf16[144,384]{1,0:T(8,128)(2,1)}), bf16[2304,384]{1,0:T(8,128)(2,1)}) %all-gather.2.cloned.1.call-update) | async-done | bytes 1769488 | tf_op jit(solution)/shard_map/all_gather | solution.py:75
  143.1 11.6 %fusion.31 = f32[2304,384]{1,0:T(8,128)} fusion(bf16[1024,2304]{1,0:T(8,128)(2,1)} %constant_dynamic-update-slice_fusion, bf16[1024,384]{1,0:T(8,128)(2,1)S(1)} %bitcast.97, bf16[2304,384]{1,0:T(8,128)(2,1)} %all-gather.2.cloned.1.call-done), kind=kOutput, calls=%fused_computation.36 | convolution fusion | flops 3632136192 | bytes 10813440 | tf_op jit(solution)/shard_map/dot_general | solution.py:82
  154.8 212.2 %reduce-scatter.2.cloned.1.call-done = f32[144,384]{1,0:T(8,128)} async-done(((f32[2304,384]{1,0:T(8,128)}), f32[144,384]{1,0:T(8,128)}) %reduce-scatter.2.cloned.1.call-update) | async-done | bytes 221200 | tf_op jit(solution)/shard_map/reduce_scatter | solution.py:86
  367.0 227.2 %all-reduce.2.cloned.1.call-done = f32[144,384]{1,0:T(8,128)} async-done(((f32[144,384]{1,0:T(8,128)}), f32[144,384]{1,0:T(8,128)}) %all-reduce.2.cloned.1.call-update) | async-done | bytes 221200 | tf_op jit(solution)/shard_map/psum | solution.py:85
  594.2 1.6 copy.32
  (35 shorter events, 9.0 us)
Async XLA Ops:
  6.5 29.6 %copy-start = (bf16[1,1024,256]{2,1,0:T(8,128)(2,1)S(1)}, bf16[1,1024,256]{2,1,0:T(8,128)(2,1)}, u32[]{:S(2)}) copy-start(bf16[1,1024,256]{2,1,0:T(8,128)(2,1)} %param.7) | copy-start | bytes 1572868
  23.3 20.7 %all-to-all-start = ((s32[32,1,128]{2,1,0:T(1,128)}), s32[32,1,128]{2,1,0:T(1,128)S(1)}, u32[]{:S(2)}, u32[]{:S(2)}) async-start(s32[32,1,128]{2,1,0:T(1,128)} %bitcast.11), calls=%async_computation | async-start | bytes 32768 | tf_op jit(solution)/shard_map/all_to_all | solution.py:48
  43.9 57.2 %all-to-all-start.1 = ((bf16[32,128,256]{2,1,0:T(8,128)(2,1)}), bf16[32,128,256]{2,1,0:T(8,128)(2,1)S(1)}, u32[]{:S(2)}, u32[]{:S(2)}) async-start(bf16[32,128,256]{2,1,0:T(8,128)(2,1)} %bitcast.14), calls=%async_computation.1 | async-start | bytes 4194304 | tf_op jit(solution)/shard_map/all_to_all | solution.py:41
  51.1 92.0 %all-gather.2.cloned.1.call-start = ((), (), s32[]{:S(2)}) async-start(), calls=%async_computation.3 | async-start | bytes 1880064 | tf_op jit(solution)/shard_map/all_gather | solution.py:75
  51.8 315.1 %reduce-scatter.2.cloned.1.call-start = ((), (), s32[]{:S(2)}) async-start(), calls=%async_computation.4 | async-start | bytes 3760128 | tf_op jit(solution)/shard_map/reduce_scatter | solution.py:86
  105.9 6.4 %collective-permute-start = (bf16[1,256,256]{2,1,0:T(8,128)(2,1)S(1)}, bf16[1,256,256]{2,1,0:T(8,128)(2,1)S(1)}, u32[]{:S(2)}, u32[]{:S(2)}) collective-permute-start(bf16[1,256,256]{2,1,0:T(8,128)(2,1)S(1)} %get-tuple-element.53), channel_id=1, source_target_pairs={{0,1},{1,2},{2,3},{3,4},{4,5},{5,6},{6,7},{7,8},{8,9},{9,10},{10,1... | collective-permute-start | bytes 393224 | tf_op jit(solution)/shard_map/ppermute | solution.py:15
  109.6 9.4 %collective-permute-start.1 = (bf16[1,256,256]{2,1,0:T(8,128)(2,1)S(1)}, bf16[1,256,256]{2,1,0:T(8,128)(2,1)S(1)}, u32[]{:S(2)}, u32[]{:S(2)}) collective-permute-start(bf16[1,256,256]{2,1,0:T(8,128)(2,1)S(1)} %get-tuple-element.54), channel_id=1, source_target_pairs={{1,0},{2,1},{3,2},{4,3},{5,4},{6,5},{7,6},{8,7},{9,8},{10,9},{11,1... | collective-permute-start | bytes 393224 | tf_op jit(solution)/shard_map/ppermute | solution.py:17
  125.0 18.0 %copy-start.1 = (bf16[1,4,256,384]{3,2,1,0:T(8,128)(2,1)S(1)}, bf16[1,4,256,384]{3,2,1,0:T(8,128)(2,1)}, u32[]{:S(2)}) copy-start(bf16[1,4,256,384]{3,2,1,0:T(8,128)(2,1)} %param.11) | copy-start | bytes 2359300
  154.7 439.5 %all-reduce.2.cloned.1.call-start = ((), (), s32[]{:S(2)}) async-start(), calls=%async_computation.5 | async-start | bytes 442368 | tf_op jit(solution)/shard_map/psum | solution.py:85
Sparse Core Ops, SparseCore 0:
  55.1 87.8 all-gather.1
  154.8 212.0 reduce-scatter.1
  370.1 224.0 all-reduce.1
where the time goes:
time: 603 us; the launch traced here: 602 us
  waiting for transfers between devices  513 us (85%)
  starting transfers between devices  26 us (4%)
  local copies, waits for them, and re-layouts  21.8 us (4%)
  matrix products  14.3 us (2%)
  other arithmetic  13.7 us (2%)
  between operations  13.2 us (2%)
    psum x1, waiting for transfers between devices, local(): summed = lax.psum(full_grad, 'tile')  227 us
    reduce_scatter x1, waiting for transfers between devices, local(): result = lax.psum_scatter(summed, 'dp', scatter_dimension=0, tiled=True)  212 us
    all_to_all x1, waiting for transfers between devices, local(): lax.all_to_all(send_feat.reshape(ntiles, capacity, dobs), 'tile', split_a...  49.3 us
    all_gather x1, waiting for transfers between devices, local(): lax.all_gather(conv_weight, 'dp', axis=0, tiled=True)  15.5 us
    all_to_all x1, starting transfers between devices, local(): lax.all_to_all(send_cell.reshape(ntiles, capacity), 'tile', split_axis=0,...  12.9 us
  transfers between devices with their start and end apart: 7, of which 7 were waited for; matrix products, arithmetic and copies ran while one was open for 3% of the time, Pallas kernels for 0%

commit v1 on v0

v1 whole, which is shorter than its diff:
```python
import jax
import jax.numpy as jnp
from jax import lax
from jax.experimental import pallas as pl
from jax.experimental.pallas import tpu as pltpu
from jax.sharding import PartitionSpec as P

MESH = pl.DeviceIdType.MESH
F32 = jnp.float32
BF16 = jnp.bfloat16
NZ = 8
NY = 8
NT = 32
CAP = 128
ORDER = (4, 3, 5, 2, 6, 1, 7, 0)


def remote(src, dst, send, recv, where):
    return pltpu.make_async_remote_copy(
        src_ref=src, dst_ref=dst, send_sem=send, recv_sem=recv,
        device_id=where, device_id_type=MESH,
    )


def arrived(ref, sem, me):
    remote(ref, ref, sem, sem, me).wait_recv()


def front(rec_ref, tile_ref, cell_ref, w_ref, cot_ref, g_ref,
          sbuf, scell, rbuf, rcell, wbuf, xbuf, rmat, acc, dens, gp,
          rec_send, cell_send, w_send, f_send, h_send,
          rec_recv, cell_recv, w_recv, f_recv, h_recv):
    tile = lax.axis_index("tile")
    dp = lax.axis_index("dp")
    z = lax.div(tile, 4)
    kme = lax.rem(tile, 4)
    core = lax.rem(tile, 2)
    ndp = 2 * NY
    me = {"tile": tile}

    barrier = pltpu.get_barrier_semaphore()

    def greet_tile(i, _):
        pl.semaphore_signal(barrier, inc=1, device_id={"tile": lax.rem(tile + i, NT)}, device_id_type=MESH)
        return 0

    def greet_dp(i, _):
        pl.semaphore_signal(barrier, inc=1, device_id={"dp": lax.rem(dp + i, ndp)}, device_id_type=MESH)
        return 0

    lax.fori_loop(1, NT, greet_tile, 0)
    lax.fori_loop(1, ndp, greet_dp, 0)

    dest = tile_ref[...]
    marks = (lax.broadcasted_iota(jnp.int32, (NT, 1024), 0) == dest).astype(F32)
    upper = (lax.broadcasted_iota(jnp.int32, (256, 256), 0)
             < lax.broadcasted_iota(jnp.int32, (256, 256), 1)).astype(F32).astype(BF16)
    carry = jnp.zeros((NT, 1), F32)
    parts = []
    for c in range(4):
        m = marks[:, 256 * c:256 * c + 256]
        parts.append(jnp.dot(m.astype(BF16), upper, preferred_element_type=F32) + carry)
        carry = carry + jnp.sum(m, axis=1, keepdims=True)
    before = jnp.concatenate(parts, axis=1)
    pos = jnp.sum(before * marks, axis=0, keepdims=True).astype(jnp.int32)
    slot = dest * CAP + pos
    spot = (lax.broadcasted_iota(jnp.int32, (CAP, 1024), 0) == pos).astype(F32).astype(BF16)
    code = cell_ref[...] + 1
    high = jnp.right_shift(code, 5)
    low = code - high * 32
    nt = (((1,), (1,)), ((), ()))
    chigh = lax.dot_general((marks * high.astype(F32)).astype(BF16), spot, nt, preferred_element_type=F32)
    clow = lax.dot_general((marks * low.astype(F32)).astype(BF16), spot, nt, preferred_element_type=F32)
    cells = (chigh * 32.0 + clow).astype(jnp.int32) - 1
    for t in range(NT):
        scell[t] = cells[t:t + 1, :]

    def own_rows(d):
        return pl.ds(pl.multiple_of(144 * d, 16), 144)

    active = lax.rem(dp + core, 2) == 0

    @pl.when(active)
    def _():
        wbuf[own_rows(dp), :] = w_ref[...]

    pl.semaphore_wait(barrier, NT - 1 + ndp - 1)

    def w_copy(i):
        d = lax.rem(dp + i, ndp)
        return remote(w_ref, wbuf.at[own_rows(dp)], w_send.at[i], w_recv, {"dp": d})

    @pl.when(active)
    def _():
        for i in range(1, ndp):
            w_copy(i).start()

    def cell_copy(gd, k):
        t = lax.rem(z + gd, NZ) * 4 + k
        return remote(scell.at[t], rcell.at[((NZ - gd) % NZ) * 4 + kme],
                      cell_send.at[gd * 4 + k], cell_recv, {"tile": t})

    def rec_copy(gd, k):
        t = lax.rem(z + gd, NZ) * 4 + k
        g = (NZ - gd) % NZ
        return remote(sbuf.at[gd, k], rbuf.at[g, kme],
                      rec_send.at[gd * 4 + k], rec_recv.at[g], {"tile": t})

    def each(gd, act):
        for k in range(4):
            if gd == 0:
                @pl.when(k != kme)
                def _():
                    act(gd, k)
            else:
                act(gd, k)

    for gd in ORDER:
        each(gd, lambda gd, k: cell_copy(gd, k).start())

    for gd in ORDER:
        base = lax.rem(z + gd, NZ) * (4 * CAP)
        pick = (lax.broadcasted_iota(jnp.int32, (4 * CAP, 1024), 0) == (slot - base)).astype(F32).astype(BF16)
        packed = jnp.dot(pick, rec_ref[...], preferred_element_type=F32).astype(BF16)
        for k in range(4):
            sbuf[gd, k] = packed[CAP * k:CAP * k + CAP]
        each(gd, lambda gd, k: rec_copy(gd, k).start())
    rbuf[0, kme] = sbuf[0, kme]
    rcell[kme] = scell[tile]

    @pl.when(active)
    def _():
        arrived(wbuf.at[pl.ds(0, 144 * (ndp // 2 - 1))], w_recv, me)

    @pl.when(jnp.logical_not(active))
    def _():
        arrived(wbuf.at[pl.ds(0, 144 * (ndp // 2))], w_recv, me)

    partner = {"tile": tile + 1 - 2 * core}

    def f_copy(i):
        rows = own_rows(2 * i + core)
        return remote(wbuf.at[rows], wbuf.at[rows], f_send.at[i], f_recv, partner)

    for i in range(ndp // 2):
        f_copy(i).start()

    arrived(rcell.at[pl.ds(0, NT - 1)], cell_recv, me)
    acc[...] = jnp.zeros_like(acc)
    dens[...] = jnp.zeros_like(dens)
    ones = jnp.ones((4 * CAP, 128), BF16)
    for gd in ORDER:
        g = (NZ - gd) % NZ
        if g == 0:
            arrived(rbuf.at[0, pl.ds(0, 3)], rec_recv.at[0], me)
        else:
            arrived(rbuf.at[g], rec_recv.at[g], me)
        ids = jnp.concatenate([rcell[4 * g + k] for k in range(4)], axis=1)

        def chunk(r, _, g=g, ids=ids):
            start = pl.multiple_of(r * 256, 256)
            hit = (lax.broadcasted_iota(jnp.int32, (256, 4 * CAP), 0) + start == ids).astype(F32).astype(BF16)
            rows = pl.ds(start, 256)
            acc[rows, :] += jnp.dot(hit, rbuf[g].reshape(4 * CAP, 256), preferred_element_type=F32)
            dens[rows, :] += jnp.dot(hit, ones, preferred_element_type=F32)
            return 0

        lax.fori_loop(0, 4, chunk, 0)

    def spread(e, value):
        rmat[pl.ds(e * 256, 256), 0:256] = pltpu.roll(value, 1, 0).astype(BF16)
        rmat[pl.ds(e * 256, 256), 256:512] = value.astype(BF16)
        rmat[pl.ds(e * 256, 256), 512:768] = pltpu.roll(value, 255, 0).astype(BF16)

    def up_copy():
        return remote(xbuf.at[1], xbuf.at[5], h_send.at[0], h_recv.at[1], {"tile": tile - 1})

    def down_copy():
        return remote(xbuf.at[4], xbuf.at[0], h_send.at[1], h_recv.at[0], {"tile": tile + 1})

    first, last = tile == 0, tile == NT - 1

    def finish(r):
        inv = 1.0 / (dens[256 * r:256 * r + 256, :] + 1.0)
        value = acc[256 * r:256 * r + 256, :] * jnp.concatenate([inv, inv], axis=1)
        xbuf[r + 1] = value.astype(BF16)

    finish(0)

    @pl.when(jnp.logical_not(first))
    def _():
        up_copy().start()

    finish(3)

    @pl.when(jnp.logical_not(last))
    def _():
        down_copy().start()

    finish(1)
    finish(2)
    for e in range(1, 5):
        spread(e, xbuf[e].astype(F32))
    arrived(wbuf.at[pl.ds(0, 144 * (ndp // 2))], f_recv, me)

    def conv(r, n):
        pre = jnp.zeros((256 * n, 384), F32)
        for p in range(3):
            pre = pre + jnp.dot(rmat[256 * (r + p):256 * (r + p + n), :], wbuf[768 * p:768 * p + 768, :],
                                preferred_element_type=F32)
        c0 = 0.7978845608028654
        sq = pre * pre
        th = jnp.tanh(c0 * pre * (1.0 + 0.044715 * sq))
        slope = 0.5 * (1.0 + th) + 0.5 * pre * (1.0 - th * th) * (c0 * (1.0 + 3.0 * 0.044715 * sq))
        gp[256 * r:256 * (r + n), :] = (cot_ref[256 * r:256 * (r + n), :].astype(F32) * slope).astype(BF16)

    conv(1, 2)

    @pl.when(first)
    def _():
        xbuf[0] = jnp.zeros((256, 256), BF16)

    @pl.when(last)
    def _():
        xbuf[5] = jnp.zeros((256, 256), BF16)

    @pl.when(jnp.logical_not(first))
    def _():
        arrived(xbuf.at[0], h_recv.at[0], me)

    @pl.when(jnp.logical_not(last))
    def _():
        arrived(xbuf.at[5], h_recv.at[1], me)

    spread(0, xbuf[0].astype(F32))
    spread(5, xbuf[5].astype(F32))
    conv(0, 1)
    conv(3, 1)
    tn = (((0,), (0,)), ((), ()))
    for p in range(3):
        for q in range(3):
            g_ref[256 * (3 * p + q):256 * (3 * p + q) + 256, :] = lax.dot_general(
                rmat[256 * p:256 * p + 1024, 256 * q:256 * q + 256], gp[...], tn, preferred_element_type=F32)

    for gd in ORDER:
        each(gd, lambda gd, k: (cell_copy(gd, k).wait_send(), rec_copy(gd, k).wait_send()))

    @pl.when(active)
    def _():
        for i in range(1, ndp):
            w_copy(i).wait_send()

    for i in range(ndp // 2):
        f_copy(i).wait_send()

    @pl.when(jnp.logical_not(first))
    def _():
        up_copy().wait_send()

    @pl.when(jnp.logical_not(last))
    def _():
        down_copy().wait_send()


def reduce(g_ref, out_ref, s1, r1, s2, ra2, rb2, pa3, pb3, ra3, rb3, qa, qb, qf, ra4, rb4, f5,
           sends, recvs):
    tile = lax.axis_index("tile")
    dp = lax.axis_index("dp")
    z = lax.div(tile, 4)
    xlo = lax.rem(lax.div(tile, 2), 2)
    c = lax.rem(tile, 2)
    y = lax.rem(dp, NY)
    xhi = lax.div(dp, NY)
    x = xhi * 2 + xlo
    me = {"tile": tile}

    def at(xx, yy, zz, cc):
        return {"dp": lax.div(xx, 2) * NY + yy, "tile": zz * 4 + lax.rem(xx, 2) * 2 + cc}

    nsend = [0]
    started = []

    def send(cond, src, dst, recv, where):
        n = nsend[0]
        nsend[0] += 1

        def copy():
            return remote(src, dst, sends.at[n], recv, where)

        started.append((cond, copy))
        if cond is None:
            copy().start()
        else:
            @pl.when(cond)
            def _():
                copy().start()

    barrier = pltpu.get_barrier_semaphore()

    def greet(where):
        pl.semaphore_signal(barrier, inc=1, device_id=where, device_id_type=MESH)

    greet(at(x, y, z, 1 - c))
    for i in range(1, NY):
        greet(at(x, lax.rem(y + i, NY), z, c))
        greet(at(x, y, lax.rem(z + i, NZ), c))
    for i in range(1, 4):
        greet(at(lax.rem(x + i, 4), y, z, c))
    cross = lax.rem(y + c, 2) == 0
    for i in range(NY):
        yy = (y + i) % NY

        @pl.when(jnp.logical_not((yy == y) & (y == z)))
        def _(yy=yy):
            greet(at(x, yy, y, c))

    def shard(m, cc):
        h, jj = m // 4, m % 4
        return pl.ds(pl.multiple_of(144 * (NY * h + 2 * jj + cc), 16), 144)

    for m in range(8):
        s1[m] = g_ref[shard(m, 1 - c), :].astype(BF16)
    pl.semaphore_wait(barrier, 1 + 2 * (NY - 1) + 3 + NY - (y == z).astype(jnp.int32))
    for m in range(8):
        send(None, s1.at[m], r1.at[m], recvs.at[0, m], at(x, y, z, 1 - c))
    mine_a = lax.rem(y + c, 2) == 0
    mine_b = lax.rem(z + c, 2) == 0
    for jj in range(4):
        for h in range(2):
            m = 4 * h + jj
            arrived(r1.at[m], recvs.at[0, m], me)
            s2[m] = (g_ref[shard(m, c), :] + r1[m].astype(F32)).astype(BF16)
            j = 2 * jj + c
            if h == 0:
                send(j != y, s2.at[m], ra2.at[y], recvs.at[1, 0], at(x, j, z, c))

                @pl.when(j == y)
                def _(m=m):
                    ra2[y] = s2[m]
            else:
                send(j != z, s2.at[m], rb2.at[z], recvs.at[1, 1], at(x, y, j, c))

                @pl.when(j == z)
                def _(m=m):
                    rb2[z] = s2[m]

    def pieces(src, dst):
        total = src[0].astype(F32)
        for i in range(1, 8):
            total = total + src[i].astype(F32)
        stack = jnp.concatenate([total[:, 128 * b:128 * b + 128] for b in range(3)], axis=0)
        for k in range(8):
            dst[k, 0:54] = stack[54 * k:54 * k + 54]
            dst[k, 54:56] = jnp.zeros((2, 128), F32)

    @pl.when(mine_a)
    def _():
        arrived(ra2.at[pl.ds(0, 7)], recvs.at[1, 0], me)
        pieces(ra2, pa3)
        ra3[z] = pa3[z]

    for i in range(1, 8):
        zz = lax.rem(z + i, NZ)
        send(mine_a, pa3.at[zz], ra3.at[z], recvs.at[2, 0], at(x, y, zz, c))

    @pl.when(mine_b)
    def _():
        arrived(rb2.at[pl.ds(0, 7)], recvs.at[1, 1], me)
        pieces(rb2, pb3)
        rb3[y] = pb3[y]

    for i in range(1, 8):
        yy = lax.rem(y + i, NY)
        send(mine_b, pb3.at[yy], rb3.at[y], recvs.at[2, 1], at(x, yy, z, c))

    def total(src, n):
        t = src[0]
        for i in range(1, n):
            t = t + src[i]
        return t

    here_a = mine_a & (xhi == 0)
    here_b = mine_b & (xhi == 1)

    @pl.when(mine_a)
    def _():
        arrived(ra3.at[pl.ds(0, 7)], recvs.at[2, 0], me)
        qa[...] = total(ra3, 8)

    for i in range(2):
        send(mine_a & (x != i), qa, ra4.at[x], recvs.at[3, 0], at(jnp.int32(i), y, z, c))

    @pl.when(mine_b)
    def _():
        arrived(rb3.at[pl.ds(0, 7)], recvs.at[2, 1], me)
        qb[...] = total(rb3, 8)

    for i in range(2, 4):
        send(mine_b & (x != i), qb, rb4.at[x], recvs.at[3, 1], at(jnp.int32(i), y, z, c))

    @pl.when(here_a)
    def _():
        ra4[x] = qa[...]
        arrived(ra4.at[pl.ds(0, 3)], recvs.at[3, 0], me)
        f5[z] = total(ra4, 4)

    for i in range(1, 8):
        zz = lax.rem(z + i, NZ)
        send(here_a, f5.at[z], f5.at[z], recvs.at[4, 0], at(x, y, zz, c))

    @pl.when(here_b)
    def _():
        rb4[x] = qb[...]
        arrived(rb4.at[pl.ds(0, 3)], recvs.at[3, 1], me)
        qf[...] = total(rb4, 4)

    for i in range(8):
        zz = lax.rem(z + i, NZ)
        away = jnp.logical_not((y == z) & (zz == z))
        send(here_b & away, qf, f5.at[y], recvs.at[4, 1], at(x, z, zz, c))

    @pl.when(here_b & (y == z))
    def _():
        f5[y] = qf[...]

    @pl.when(here_a)
    def _():
        arrived(f5.at[pl.ds(0, 7)], recvs.at[4, 0], me)

    owner_b = mine_a & (xhi == 1)

    @pl.when(owner_b & (y == z))
    def _():
        arrived(f5.at[pl.ds(0, 7)], recvs.at[4, 1], me)

    @pl.when(owner_b & (y != z))
    def _():
        arrived(f5, recvs.at[4, 1], me)

    send(mine_a, f5, f5, recvs.at[5, 0], at(x, y, z, 1 - c))

    @pl.when(jnp.logical_not(mine_a))
    def _():
        arrived(f5, recvs.at[5, 0], me)

    stack = jnp.concatenate([f5[k, 0:54] for k in range(8)], axis=0)
    for b in range(3):
        out_ref[:, 128 * b:128 * b + 128] = stack[144 * b:144 * b + 144]

    for cond, copy in started:
        if cond is None:
            copy().wait_send()
        else:
            @pl.when(cond)
            def _(copy=copy):
                copy().wait_send()


def local(records, obs_tile, obs_cell, conv_weight, cotangent):
    vm = pl.BlockSpec(memory_space=pltpu.VMEM)
    dma = pltpu.SemaphoreType.DMA
    grad = pl.pallas_call(
        front,
        out_shape=jax.ShapeDtypeStruct((2304, 384), F32),
        in_specs=[vm] * 5,
        out_specs=vm,
        scratch_shapes=[
            pltpu.VMEM((NZ, 4, CAP, 256), BF16),
            pltpu.VMEM((NT, 1, CAP), jnp.int32),
            pltpu.VMEM((NZ, 4, CAP, 256), BF16),
            pltpu.VMEM((NT, 1, CAP), jnp.int32),
            pltpu.VMEM((2304, 384), BF16),
            pltpu.VMEM((6, 256, 256), BF16),
            pltpu.VMEM((1536, 768), BF16),
            pltpu.VMEM((1024, 256), F32),
            pltpu.VMEM((1024, 128), F32),
            pltpu.VMEM((1024, 384), BF16),
            dma((NT,)), dma((NT,)), dma((2 * NY,)), dma((NY,)), dma((2,)),
            dma((NZ,)), dma, dma, dma, dma((2,)),
        ],
        compiler_params=pltpu.CompilerParams(
            collective_id=0, has_side_effects=True, vmem_limit_bytes=50 * 1024 * 1024),
    )(records[0], obs_tile.reshape(1, 1024), obs_cell, conv_weight, cotangent.reshape(1024, 384))
    block = pltpu.VMEM((8, 144, 384), BF16)
    small = pltpu.VMEM((8, 56, 128), F32)
    piece = pltpu.VMEM((56, 128), F32)
    quad = pltpu.VMEM((4, 56, 128), F32)
    return pl.pallas_call(
        reduce,
        out_shape=jax.ShapeDtypeStruct((144, 384), F32),
        in_specs=[vm],
        out_specs=vm,
        scratch_shapes=[block] * 5 + [small] * 4 + [piece] * 3 + [quad] * 2 + [small, dma((64,)), dma((6, 8))],
        compiler_params=pltpu.CompilerParams(
            collective_id=1, has_side_effects=True, vmem_limit_bytes=50 * 1024 * 1024),
    )(grad)


def solution(mesh):
    placed = (
        P("dp", "tile", None),
        P("dp", "tile", None),
        P("dp", "tile"),
        P("dp", None),
        P("dp", "tile", None, None),
    )
    return jax.shard_map(
        local, mesh=mesh, in_specs=placed, out_specs=P("dp", None), check_vma=False
    )
```

time: 603 us -> 131 us (0.22)
  the two profiles are of different devices: /device:TPU:1 before, /device:TPU:37 now
where the time goes in v1:
time: 131 us
  Pallas kernels  123 us (94%)
  local copies, waits for them, and re-layouts  7.12 us (5%)
    pallas_call x1, Pallas kernels, local(): pl.pallas_call(front, out_shape=jax.ShapeDtypeStruct((2304, 384), F32), i...  73.9 us
    pallas_call x1, Pallas kernels, local(): pl.pallas_call(reduce, out_shape=jax.ShapeDtypeStruct((144, 384), F32), i...  49.5 us
    unnamed x13, local copies, waits for them, and re-layouts  7.12 us

profile of v1, /device:TPU:37, one launch (start us, length us, event | category | flops | bytes accessed | tf_op | source)
XLA Modules:
  0.0 130.6 jit_solution(8208997571268937551)
XLA Ops:
  0.0 0.0 copy-start.1
  0.0 1.1 copy-done.1
  1.1 0.0 copy-start.2
  1.1 1.0 copy-done.2
  2.2 0.0 copy-start.3
  2.2 0.9 copy-done.3
  3.1 0.0 copy-start.4
  3.1 0.7 copy-done.4
  3.8 0.0 copy-start.5
  3.8 0.7 copy-done.5
  4.4 73.9 %shard_map.55.g_ref = f32[2304,384]{1,0:T(8,128)} custom-call(bf16[1024,256]{1,0:T(8,128)(2,1)S(1)} %bitcast.4, s32[1,1024]{1,0:T(1,128)S(1)} %bitcast.5, s32[1,1024]{1,0:T(1,128)S(1)} %copy-done.5, bf16[144,384]{1,0:T(8,128)(2,1)S(1)} %copy-done.3, bf16[1024,384]{1,0:T(8,128)(2,1)S(1)} %bitcast.3), custom_call_target="tpu_custom_call" | custom-call | tf_op jit(solution)/shard_map/pallas_call | solution.py:462
  78.4 0.0 copy-start
  78.4 2.0 %copy-done = f32[2304,384]{1,0:T(8,128)S(1)} copy-done((f32[2304,384]{1,0:T(8,128)S(1)}, f32[2304,384]{1,0:T(8,128)}, u32[]{:S(2)}) %copy-start) | copy-done | bytes 3538968
  80.4 49.5 %shard_map.56 = f32[144,384]{1,0:T(8,128)S(1)} custom-call(f32[2304,384]{1,0:T(8,128)S(1)} %copy-done), custom_call_target="tpu_custom_call" | custom-call | tf_op jit(solution)/shard_map/pallas_call | solution.py:488
  129.9 0.7 copy.7
Async XLA Ops:
  0.0 1.1 copy-start.1
  1.1 1.0 copy-start.2
  2.2 0.9 copy-start.3
  3.1 0.7 copy-start.4
  3.8 0.7 copy-start.5
  78.4 2.0 %copy-start = (f32[2304,384]{1,0:T(8,128)S(1)}, f32[2304,384]{1,0:T(8,128)}, u32[]{:S(2)}) copy-start(f32[2304,384]{1,0:T(8,128)} %shard_map.55.g_ref) | copy-start | bytes 10616836

commit v2 on v0

v2 whole, which is shorter than its diff:
```python
import jax
import jax.numpy as jnp
from jax import lax
from jax.experimental import pallas as pl
from jax.experimental.pallas import tpu as pltpu
from jax.sharding import PartitionSpec as P

MESH = pl.DeviceIdType.MESH
F32 = jnp.float32
BF16 = jnp.bfloat16
NZ = 8
NY = 8
NT = 32
CAP = 128
ORDER = (0, 1, 7, 2, 6, 3, 5, 4)


def remote(src, dst, send, recv, where):
    return pltpu.make_async_remote_copy(
        src_ref=src, dst_ref=dst, send_sem=send, recv_sem=recv,
        device_id=where, device_id_type=MESH,
    )


def fused(rec_hbm, tile_hbm, cell_hbm, w_hbm, cot_hbm, out_ref,
          rec, til, cel, wloc, cot,
          sbuf, scell, rbuf, rcell, wbuf, xbuf, rmat, acc, dens, gp, grad,
          s1, r1, s2a, s2b, ra2, rb2, pa3, pb3, ra3, rb3, q4, r4, f5,
          local_sem, sends, rec_recv, cell_recv, w_recv, f_recv, h_recv, recvs):
    tile = lax.axis_index("tile")
    dp = lax.axis_index("dp")
    z = lax.div(tile, 4)
    kme = lax.rem(tile, 4)
    xlo = lax.div(kme, 2)
    c = lax.rem(tile, 2)
    y = lax.rem(dp, NY)
    xhi = lax.div(dp, NY)
    x = xhi * 2 + xlo
    ndp = 2 * NY
    me = {"tile": tile}

    def at(xx, yy, zz, cc):
        return {"dp": lax.div(xx, 2) * NY + yy, "tile": zz * 4 + lax.rem(xx, 2) * 2 + cc}

    def arrived(ref, sem):
        remote(ref, ref, sem, sem, me).wait_recv()

    started = []

    def under(cond, act):
        if cond is None:
            act()
        else:
            pl.when(cond)(act)

    def send(cond, src, dst, recv, where):
        n = len(started)

        def copy():
            return remote(src, dst, sends.at[n], recv, where)

        started.append((cond, copy))
        under(cond, lambda: copy().start())

    barrier = pltpu.get_barrier_semaphore()

    def greet(where):
        pl.semaphore_signal(barrier, inc=1, device_id=where, device_id_type=MESH)

    def greet_tile(i, _):
        greet({"tile": lax.rem(tile + i, NT)})
        return 0

    def greet_dp(i, _):
        greet({"dp": lax.rem(dp + i, ndp)})
        return 0

    loads = [pltpu.make_async_copy(a, b, local_sem.at[i]) for i, (a, b) in enumerate(
        ((tile_hbm, til), (cell_hbm, cel), (rec_hbm, rec), (w_hbm, wloc), (cot_hbm, cot)))]
    for load in loads:
        load.start()
    lax.fori_loop(1, NT, greet_tile, 0)
    lax.fori_loop(1, ndp, greet_dp, 0)
    greet(at(3 - 2 * xhi - xlo, y, z, c))
    loads[0].wait()
    loads[1].wait()

    dest = til[...]
    marks = (lax.broadcasted_iota(jnp.int32, (NT, 1024), 0) == dest).astype(F32)
    upper = (lax.broadcasted_iota(jnp.int32, (256, 256), 0)
             < lax.broadcasted_iota(jnp.int32, (256, 256), 1)).astype(F32).astype(BF16)
    carry = jnp.zeros((NT, 1), F32)
    parts = []
    for i in range(4):
        m = marks[:, 256 * i:256 * i + 256]
        parts.append(jnp.dot(m.astype(BF16), upper, preferred_element_type=F32) + carry)
        carry = carry + jnp.sum(m, axis=1, keepdims=True)
    before = jnp.concatenate(parts, axis=1)
    pos = jnp.sum(before * marks, axis=0, keepdims=True).astype(jnp.int32)
    slot = dest * CAP + pos
    spot = (lax.broadcasted_iota(jnp.int32, (CAP, 1024), 0) == pos).astype(F32).astype(BF16)
    code = cel[...] + 1
    high = jnp.right_shift(code, 5)
    low = code - high * 32
    nt = (((1,), (1,)), ((), ()))
    chigh = lax.dot_general((marks * high.astype(F32)).astype(BF16), spot, nt, preferred_element_type=F32)
    clow = lax.dot_general((marks * low.astype(F32)).astype(BF16), spot, nt, preferred_element_type=F32)
    cells = (chigh * 32.0 + clow).astype(jnp.int32) - 1
    for t in range(NT):
        scell[t] = cells[t:t + 1, :]

    loads[2].wait()
    for gd in ORDER:
        base = lax.rem(z + gd, NZ) * (4 * CAP)
        pick = (lax.broadcasted_iota(jnp.int32, (4 * CAP, 1024), 0) == (slot - base)).astype(F32).astype(BF16)
        packed = jnp.dot(pick, rec[...], preferred_element_type=F32).astype(BF16)
        for k in range(4):
            sbuf[gd, k] = packed[CAP * k:CAP * k + CAP]
    loads[3].wait()

    def own_rows(d):
        return pl.ds(pl.multiple_of(144 * d, 16), 144)

    active = lax.rem(dp + c, 2) == 0
    pl.semaphore_wait(barrier, NT - 1 + ndp - 1 + 1)

    for gd in ORDER:
        t = lax.rem(z + gd, NZ) * 4
        g = (NZ - gd) % NZ
        for k in range(4):
            away = (k != kme) if gd == 0 else None
            send(away, scell.at[t + k], rcell.at[g * 4 + kme], cell_recv, {"tile": t + k})
            send(away, sbuf.at[gd, k], rbuf.at[g, kme], rec_recv.at[g], {"tile": t + k})
    for i in range(1, ndp):
        send(active, wloc, wbuf.at[own_rows(dp)], w_recv, {"dp": lax.rem(dp + i, ndp)})
    rbuf[0, kme] = sbuf[0, kme]
    rcell[kme] = scell[tile]

    @pl.when(active)
    def _():
        wbuf[own_rows(dp), :] = wloc[...]
        arrived(wbuf.at[pl.ds(0, 144 * (ndp // 2 - 1))], w_recv)

    @pl.when(jnp.logical_not(active))
    def _():
        arrived(wbuf.at[pl.ds(0, 144 * (ndp // 2))], w_recv)

    partner = at(x, y, z, 1 - c)
    for i in range(ndp // 2):
        rows = own_rows(2 * i + c)
        send(None, wbuf.at[rows], wbuf.at[rows], f_recv, partner)

    arrived(rcell.at[pl.ds(0, NT - 1)], cell_recv)
    acc[...] = jnp.zeros_like(acc)
    dens[...] = jnp.zeros_like(dens)
    ones = jnp.ones((4 * CAP, 128), BF16)

    def chunk(g, ids, start):
        hit = (lax.broadcasted_iota(jnp.int32, (256, 4 * CAP), 0) + start == ids).astype(F32).astype(BF16)
        rows = pl.ds(start, 256)
        acc[rows, :] += jnp.dot(hit, rbuf[g].reshape(4 * CAP, 256), preferred_element_type=F32)
        dens[rows, :] += jnp.dot(hit, ones, preferred_element_type=F32)

    def group(gd):
        g = (NZ - gd) % NZ
        if g == 0:
            arrived(rbuf.at[0, pl.ds(0, 3)], rec_recv.at[0])
        else:
            arrived(rbuf.at[g], rec_recv.at[g])
        return g, jnp.concatenate([rcell[4 * g + k] for k in range(4)], axis=1)

    for gd in ORDER[:-1]:
        g, ids = group(gd)

        def step(r, _, g=g, ids=ids):
            chunk(g, ids, pl.multiple_of(r * 256, 256))
            return 0

        lax.fori_loop(0, 4, step, 0)

    def spread(e):
        value = xbuf[e].astype(F32)
        rmat[pl.ds(e * 256, 256), 0:256] = pltpu.roll(value, 1, 0).astype(BF16)
        rmat[pl.ds(e * 256, 256), 256:512] = value.astype(BF16)
        rmat[pl.ds(e * 256, 256), 512:768] = pltpu.roll(value, 255, 0).astype(BF16)

    first, last = tile == 0, tile == NT - 1
    inner_top, inner_end = jnp.logical_not(first), jnp.logical_not(last)

    def finish(r):
        inv = 1.0 / (dens[256 * r:256 * r + 256, :] + 1.0)
        value = acc[256 * r:256 * r + 256, :] * jnp.concatenate([inv, inv], axis=1)
        xbuf[r + 1] = value.astype(BF16)

    g, ids = group(ORDER[-1])
    chunk(g, ids, 0)
    finish(0)
    send(inner_top, xbuf.at[1], xbuf.at[5], h_recv.at[1], {"tile": tile - 1})
    chunk(g, ids, 768)
    finish(3)
    send(inner_end, xbuf.at[4], xbuf.at[0], h_recv.at[0], {"tile": tile + 1})
    chunk(g, ids, 256)
    chunk(g, ids, 512)
    finish(1)
    finish(2)
    for e in range(1, 5):
        spread(e)
    arrived(wbuf.at[pl.ds(0, 144 * (ndp // 2))], f_recv)
    loads[4].wait()

    def conv(r, n):
        pre = jnp.zeros((256 * n, 384), F32)
        for p in range(3):
            pre = pre + jnp.dot(rmat[256 * (r + p):256 * (r + p + n), :], wbuf[768 * p:768 * p + 768, :],
                                preferred_element_type=F32)
        c0 = 0.7978845608028654
        sq = pre * pre
        th = jnp.tanh(c0 * pre * (1.0 + 0.044715 * sq))
        slope = 0.5 * (1.0 + th) + 0.5 * pre * (1.0 - th * th) * (c0 * (1.0 + 3.0 * 0.044715 * sq))
        gp[256 * r:256 * (r + n), :] = (cot[256 * r:256 * (r + n), :].astype(F32) * slope).astype(BF16)

    tn = (((0,), (0,)), ((), ()))

    def outer(r, n, p, q):
        return lax.dot_general(
            rmat[256 * (r + p):256 * (r + p + n), 256 * q:256 * q + 256], gp[256 * r:256 * (r + n), :],
            tn, preferred_element_type=F32)

    conv(1, 2)
    for p in range(3):
        for q in range(3):
            grad[256 * (3 * p + q):256 * (3 * p + q) + 256, :] = outer(1, 2, p, q)

    @pl.when(first)
    def _():
        xbuf[0] = jnp.zeros((256, 256), BF16)

    @pl.when(last)
    def _():
        xbuf[5] = jnp.zeros((256, 256), BF16)

    @pl.when(inner_top)
    def _():
        arrived(xbuf.at[0], h_recv.at[0])

    @pl.when(inner_end)
    def _():
        arrived(xbuf.at[5], h_recv.at[1])

    spread(0)
    spread(5)
    conv(0, 1)
    conv(3, 1)

    for p in range(3):
        for q in range(3):
            grad[256 * (3 * p + q):256 * (3 * p + q) + 256, :] += outer(0, 1, p, q) + outer(3, 1, p, q)
        for k in ((0, 1), (2, 3, 4), (5, 6, 7))[p]:
            s1[k] = grad[own_rows(2 * k + 1 - c), :].astype(BF16)
            send(None, s1.at[k], r1.at[k], recvs.at[k], partner)

    def stacked(value):
        return jnp.concatenate([value[:, 128 * b:128 * b + 128] for b in range(3)], axis=0)

    def paired(k):
        arrived(r1.at[k], recvs.at[k])
        return stacked(grad[own_rows(2 * k + c), :] + r1[k].astype(F32)).astype(BF16)

    for jj in range(4):
        j = 2 * jj + c
        s2a[jj, 0:432] = paired(jj)
        send(j != y, s2a.at[jj, pl.ds(0, 432)], ra2.at[y, pl.ds(0, 432)], recvs.at[8], at(x, j, z, c))

        @pl.when(j == y)
        def _(jj=jj):
            ra2[y, 0:432] = s2a[jj, 0:432]

    for jj in range(4):
        s2b[jj, 0:432] = paired(4 + jj)
        s2b[jj, 432:448] = jnp.zeros((16, 128), BF16)
    for j in range(7):
        send(j != z, s2b.at[:, pl.ds(64 * j, 64)], rb2.at[z], recvs.at[9], at(x, y, j, c))

        @pl.when(j == z)
        def _(j=j):
            rb2[j] = s2b[:, 64 * j:64 * j + 64]

    mine = lax.rem(y + c, 2) == 0
    low_z = z < 7
    both = mine & low_z

    @pl.when(mine)
    def _():
        arrived(ra2.at[pl.ds(0, 7), pl.ds(0, 432)], recvs.at[8])
        total = ra2[0, 0:432].astype(F32)
        for i in range(1, 8):
            total = total + ra2[i, 0:432].astype(F32)
        pa3[0:432] = total
        pa3[432:448] = jnp.zeros((16, 128), F32)

    for j in range(7):
        send(mine & (j != z), pa3.at[pl.ds(64 * j, 64)], ra3.at[z], recvs.at[10], at(x, y, j, c))

    @pl.when(low_z)
    def _():
        arrived(rb2.at[pl.ds(0, 7)], recvs.at[9])
        total = rb2[0].astype(F32)
        for i in range(1, 8):
            total = total + rb2[i].astype(F32)
        pb3[...] = total

    for jj in range(4):
        j = 2 * jj + c
        send(low_z & (j != y), pb3.at[jj], rb3.at[y], recvs.at[11], at(x, j, z, c))

        @pl.when(low_z & (j == y))
        def _(jj=jj):
            rb3[y] = pb3[jj]

    @pl.when(both)
    def _():
        ra3[z] = pa3[pl.ds(pl.multiple_of(64 * z, 64), 64)]
        arrived(ra3.at[pl.ds(0, 7)], recvs.at[10])
        total = ra3[0]
        for i in range(1, 8):
            total = total + ra3[i]
        q4[0] = total
        arrived(rb3.at[pl.ds(0, 7)], recvs.at[11])
        total = rb3[0]
        for i in range(1, 8):
            total = total + rb3[i]
        q4[1] = total
        r4[x] = q4[xhi]

    for i in range(1, 4):
        xx = lax.rem(x + i, 4)
        send(both, q4.at[lax.div(xx, 2)], r4.at[x], recvs.at[12], at(xx, y, z, c))

    @pl.when(both)
    def _():
        arrived(r4.at[pl.ds(0, 3)], recvs.at[12])
        f5[z] = (r4[0] + r4[1]) + (r4[2] + r4[3])

    for i in range(1, 8):
        send(both, f5.at[z], f5.at[z], recvs.at[13], at(x, y, lax.rem(z + i, NZ), c))

    @pl.when(both)
    def _():
        arrived(f5.at[pl.ds(0, 6)], recvs.at[13])

    @pl.when(mine & (z == 7))
    def _():
        arrived(f5, recvs.at[13])

    send(mine, f5, f5, recvs.at[14], partner)

    @pl.when(jnp.logical_not(mine))
    def _():
        arrived(f5, recvs.at[14])

    done = f5[...].reshape(448, 128)
    for b in range(3):
        out_ref[:, 128 * b:128 * b + 128] = done[144 * b:144 * b + 144]

    for cond, copy in started:
        under(cond, lambda copy=copy: copy().wait_send())


def local(records, obs_tile, obs_cell, conv_weight, cotangent):
    dma = pltpu.SemaphoreType.DMA
    any_space = pl.BlockSpec(memory_space=pl.ANY)

    def half(*shape):
        return pltpu.VMEM(shape, BF16)

    def full(*shape):
        return pltpu.VMEM(shape, F32)

    def ints(*shape):
        return pltpu.VMEM(shape, jnp.int32)

    return pl.pallas_call(
        fused,
        out_shape=jax.ShapeDtypeStruct((144, 384), F32),
        in_specs=[any_space] * 5,
        out_specs=pl.BlockSpec(memory_space=pltpu.VMEM),
        scratch_shapes=[
            half(1024, 256), ints(1, 1024), ints(1, 1024), half(144, 384), half(1024, 384),
            half(NZ, 4, CAP, 256), ints(NT, 1, CAP), half(NZ, 4, CAP, 256), ints(NT, 1, CAP),
            half(2304, 384), half(6, 256, 256), half(1536, 768), full(1024, 256), full(1024, 128),
            half(1024, 384), full(2304, 384),
            half(8, 144, 384), half(8, 144, 384), half(4, 448, 128), half(4, 448, 128),
            half(8, 448, 128), half(8, 4, 64, 128), full(448, 128), full(4, 64, 128),
            full(8, 64, 128), full(8, 64, 128), full(2, 64, 128), full(4, 64, 128), full(7, 64, 128),
            dma((5,)), dma((144,)), dma((NZ,)), dma, dma, dma, dma((2,)), dma((16,)),
        ],
        compiler_params=pltpu.CompilerParams(
            collective_id=0, has_side_effects=True, vmem_limit_bytes=58 * 1024 * 1024),
    )(records[0], obs_tile.reshape(1, 1024), obs_cell, conv_weight, cotangent.reshape(1024, 384))


def solution(mesh):
    placed = (
        P("dp", "tile", None),
        P("dp", "tile", None),
        P("dp", "tile"),
        P("dp", None),
        P("dp", "tile", None, None),
    )
    return jax.shard_map(
        local, mesh=mesh, in_specs=placed, out_specs=P("dp", None), check_vma=False
    )
```

time: 603 us -> 129 us (0.21)
  waiting for transfers between devices: 513 us -> 0 us
  Pallas kernels: 0 us -> 127 us
  starting transfers between devices: 26 us -> 0 us
  local copies, waits for them, and re-layouts: 21.8 us -> 1.64 us
  matrix products: 14.3 us -> 0 us
  other arithmetic: 13.7 us -> 0 us
  between operations: 13.2 us -> 0.01 us
    psum x1 -> x0, waiting for transfers between devices: 227 us -> none  [local(): summed = lax.psum(full_grad, 'tile')]
    reduce_scatter x1 -> x0, waiting for transfers between devices: 212 us -> none  [local(): result = lax.psum_scatter(summed, 'dp', scatter_dimension=0, tiled=True)]
    pallas_call x0 -> x1, Pallas kernels: none -> 127 us  [local(): pl.pallas_call(fused, out_shape=jax.ShapeDtypeStruct((144, 384), F32), in...]
    all_to_all x2 -> x0, waiting for transfers between devices: 50.4 us -> none  [the longest x1 49.3 us: local(): lax.all_to_all(send_feat.reshape(ntiles, capacity, dobs), 'tile', split_a...]
    all_to_all x2 -> x0, starting transfers between devices: 20 us -> none  [the longest x1 12.9 us: local(): lax.all_to_all(send_cell.reshape(ntiles, capacity), 'tile', split_axis=0,...]
    all_gather x1 -> x0, waiting for transfers between devices: 15.5 us -> none  [local(): lax.all_gather(conv_weight, 'dp', axis=0, tiled=True)]
    dot_general x3 -> x0, matrix products: 14.3 us -> none  [the longest x1 11.6 us: local(): lax.dot_general(columns, gpre, (((0,), (0,)), ((), ())), preferred_elemen...]
    scatter x2 -> x0, local copies, waits for them, and re-layouts: 11.7 us -> none  [the longest x1 6.63 us: local(): jnp.zeros((ntiles * capacity, dobs), jnp.bfloat16).at[slot].set(records[0])]
  transfers between devices with their start and end apart: 7 -> 0, of which waited for: 7 -> 0; matrix products, arithmetic and copies ran while one was open for 3% -> 0% of each run, Pallas kernels for 0% -> 0%
where the time goes in v2:
time: 129 us; the launch traced here: 128 us
  Pallas kernels  127 us (98%)
  local copies, waits for them, and re-layouts  1.64 us (1%)
    pallas_call x1, Pallas kernels, local(): pl.pallas_call(fused, out_shape=jax.ShapeDtypeStruct((144, 384), F32), in...  127 us

profile of v2, /device:TPU:1, one launch (start us, length us, event | category | flops | bytes accessed | tf_op | source)
XLA Modules:
  0.0 128.4 jit_solution(6371874168257797424)
XLA Ops:
  0.0 126.7 %shard_map.55 = f32[144,384]{1,0:T(8,128)} custom-call(bf16[1024,256]{1,0:T(8,128)(2,1)} %bitcast.4, s32[1,1024]{1,0:T(1,128)} %bitcast.5, s32[1,1024]{1,0:T(1,128)} %cell_hbm.1, bf16[144,384]{1,0:T(8,128)(2,1)} %w_hbm.1, bf16[1024,384]{1,0:T(8,128)(2,1)} %bitcast.3), custom_call_target="tpu_custom_call" | custom-call | tf_op jit(solution)/shard_map/pallas_call | solution.py:382
  126.8 1.6 %copy.7 = f32[144,384]{1,0:T(8,128)} copy(f32[144,384]{1,0:T(8,128)} %shard_map.55) | data formatting | bytes 442368

commit v3 on v2

--- a/solution.py
+++ b/solution.py
@@ -12,7 +12,6 @@
 NY = 8
 NT = 32
 CAP = 128
-ORDER = (0, 1, 7, 2, 6, 3, 5, 4)
 
 
 def remote(src, dst, send, recv, where):
@@ -24,9 +23,9 @@
 
 def fused(rec_hbm, tile_hbm, cell_hbm, w_hbm, cot_hbm, out_ref,
           rec, til, cel, wloc, cot,
-          sbuf, scell, rbuf, rcell, wbuf, xbuf, rmat, acc, dens, gp, grad,
+          lout, lmeta, h1, h2, h3, h4, m1, m2, m3, m4, sbuf, scell, rbuf, rcell, wbuf, xbuf, rmat, acc, dens, gp, grad,
           s1, r1, s2a, s2b, ra2, rb2, pa3, pb3, ra3, rb3, q4, r4, f5,
-          local_sem, sends, rec_recv, cell_recv, w_recv, f_recv, h_recv, recvs):
+          local_sem, sends, ring_recv, meta_recv, rec_recv, cell_recv, w_recv, f_recv, h_recv, recvs):
     tile = lax.axis_index("tile")
     dp = lax.axis_index("dp")
     z = lax.div(tile, 4)
@@ -67,21 +66,24 @@
     def greet(where):
         pl.semaphore_signal(barrier, inc=1, device_id=where, device_id_type=MESH)
 
-    def greet_tile(i, _):
-        greet({"tile": lax.rem(tile + i, NT)})
-        return 0
-
     def greet_dp(i, _):
         greet({"dp": lax.rem(dp + i, ndp)})
         return 0
 
+    for i in (4, 3, 5, 2, 6, 1, 7):
+        greet(at(x, y, lax.rem(z + i, NZ), c))
+    for i in range(1, 8):
+        greet(at(x, y, lax.rem(z + i, NZ), 1 - c))
+    for k in range(1, 4):
+        greet({"tile": z * 4 + lax.rem(kme + k, 4)})
+    greet({"tile": lax.rem(tile + 1, NT)})
+    greet({"tile": lax.rem(tile + NT - 1, NT)})
+    lax.fori_loop(1, ndp, greet_dp, 0)
+    greet(at(3 - 2 * xhi - xlo, y, z, c))
     loads = [pltpu.make_async_copy(a, b, local_sem.at[i]) for i, (a, b) in enumerate(
         ((tile_hbm, til), (cell_hbm, cel), (rec_hbm, rec), (w_hbm, wloc), (cot_hbm, cot)))]
     for load in loads:
         load.start()
-    lax.fori_loop(1, NT, greet_tile, 0)
-    lax.fori_loop(1, ndp, greet_dp, 0)
-    greet(at(3 - 2 * xhi - xlo, y, z, c))
     loads[0].wait()
     loads[1].wait()
 
@@ -98,59 +100,79 @@
     before = jnp.concatenate(parts, axis=1)
     pos = jnp.sum(before * marks, axis=0, keepdims=True).astype(jnp.int32)
     slot = dest * CAP + pos
-    spot = (lax.broadcasted_iota(jnp.int32, (CAP, 1024), 0) == pos).astype(F32).astype(BF16)
-    code = cel[...] + 1
-    high = jnp.right_shift(code, 5)
-    low = code - high * 32
     nt = (((1,), (1,)), ((), ()))
-    chigh = lax.dot_general((marks * high.astype(F32)).astype(BF16), spot, nt, preferred_element_type=F32)
-    clow = lax.dot_general((marks * low.astype(F32)).astype(BF16), spot, nt, preferred_element_type=F32)
-    cells = (chigh * 32.0 + clow).astype(jnp.int32) - 1
-    for t in range(NT):
-        scell[t] = cells[t:t + 1, :]
-
+
+    def key(axis, shape, way):
+        t = lax.broadcasted_iota(jnp.int32, shape, axis)
+        away = jnp.bitwise_and(jnp.right_shift(t, 2) - z, 7)
+        if way == 1:
+            away = jnp.bitwise_and(8 - away, 7)
+        limit = jnp.where(jnp.bitwise_and(t, 1) == way, 4, 3)
+        return jnp.where((away >= 1) & (away <= limit), away * NT + t, -1)
+
+    total_b = jnp.broadcast_to(carry, (NT, 128)).astype(BF16)
+    spots = []
+    for way in range(2):
+        down, across = key(0, (NT, NT), way), key(1, (NT, NT), way)
+        later = (across > down).astype(F32).astype(BF16)
+        offset = jnp.dot(later, total_b, preferred_element_type=F32)[:, 0:1]
+        base = jnp.where(key(0, (NT, 1), way) >= 0, 1024.0 - offset - carry, -4096.0)
+        spots.append(jnp.sum((base + before) * marks, axis=0, keepdims=True).astype(jnp.int32))
+    code = slot + 1
+    cell = cel[...]
+    traits = jnp.concatenate([
+        jnp.right_shift(code, 6).astype(F32), jnp.bitwise_and(code, 63).astype(F32),
+        jnp.right_shift(cell, 5).astype(F32), jnp.bitwise_and(cell, 31).astype(F32),
+        jnp.zeros((4, 1024), F32)], axis=0).astype(BF16)
     loads[2].wait()
-    for gd in ORDER:
-        base = lax.rem(z + gd, NZ) * (4 * CAP)
-        pick = (lax.broadcasted_iota(jnp.int32, (4 * CAP, 1024), 0) == (slot - base)).astype(F32).astype(BF16)
-        packed = jnp.dot(pick, rec[...], preferred_element_type=F32).astype(BF16)
-        for k in range(4):
-            sbuf[gd, k] = packed[CAP * k:CAP * k + CAP]
-    loads[3].wait()
 
     def own_rows(d):
         return pl.ds(pl.multiple_of(144 * d, 16), 144)
 
     active = lax.rem(dp + c, 2) == 0
-    pl.semaphore_wait(barrier, NT - 1 + ndp - 1 + 1)
-
-    for gd in ORDER:
-        t = lax.rem(z + gd, NZ) * 4
-        g = (NZ - gd) % NZ
-        for k in range(4):
-            away = (k != kme) if gd == 0 else None
-            send(away, scell.at[t + k], rcell.at[g * 4 + kme], cell_recv, {"tile": t + k})
-            send(away, sbuf.at[gd, k], rbuf.at[g, kme], rec_recv.at[g], {"tile": t + k})
+    ahead = ({"tile": lax.rem(tile + 4, NT)}, {"tile": lax.rem(tile + NT - 4, NT)})
+    for i in (3, 2, 1, 0):
+        for way in range(2):
+            rows = pl.ds(256 * i, 256)
+            perm = (lax.broadcasted_iota(jnp.int32, (256, 1024), 0) + 256 * i == spots[way]).astype(F32).astype(BF16)
+            lout[way, rows] = jnp.dot(perm, rec[...], preferred_element_type=F32).astype(BF16)
+            got = lax.dot_general(traits, perm, nt, preferred_element_type=F32)
+            number = (got[0:1] * 64.0 + got[1:2]).astype(jnp.int32) - 1
+            lmeta[way, :, rows] = number * 1024 + (got[2:3] * 32.0 + got[3:4]).astype(jnp.int32)
+            if i == 3 and way == 0:
+                pl.semaphore_wait(barrier, 14 + 3 + 2 + ndp - 1 + 1)
+            send(None, lout.at[way, rows], h1.at[way, rows], ring_recv.at[way, i], ahead[way])
+    for way in range(2):
+        send(None, lmeta.at[way], m1.at[way], meta_recv.at[way, 0], ahead[way])
+    loads[3].wait()
     for i in range(1, ndp):
         send(active, wloc, wbuf.at[own_rows(dp)], w_recv, {"dp": lax.rem(dp + i, ndp)})
-    rbuf[0, kme] = sbuf[0, kme]
-    rcell[kme] = scell[tile]
-
-    @pl.when(active)
-    def _():
-        wbuf[own_rows(dp), :] = wloc[...]
-        arrived(wbuf.at[pl.ds(0, 144 * (ndp // 2 - 1))], w_recv)
-
-    @pl.when(jnp.logical_not(active))
-    def _():
-        arrived(wbuf.at[pl.ds(0, 144 * (ndp // 2))], w_recv)
-
-    partner = at(x, y, z, 1 - c)
-    for i in range(ndp // 2):
-        rows = own_rows(2 * i + c)
-        send(None, wbuf.at[rows], wbuf.at[rows], f_recv, partner)
-
-    arrived(rcell.at[pl.ds(0, NT - 1)], cell_recv)
+    def share(g, data, number, cell_id):
+        length = number.shape[1]
+        rel = number - 512 * z
+        pick = (lax.broadcasted_iota(jnp.int32, (4 * CAP, length), 0) == rel).astype(F32).astype(BF16)
+        packed = jnp.dot(pick, data, preferred_element_type=F32).astype(BF16)
+        owner = (lax.broadcasted_iota(jnp.int32, (8, length), 0) == jnp.right_shift(rel, 7)).astype(F32)
+        spot = (lax.broadcasted_iota(jnp.int32, (CAP, length), 0) == jnp.bitwise_and(rel, 127)).astype(F32).astype(BF16)
+        cell_code = cell_id + 1
+        high = jnp.right_shift(cell_code, 5).astype(F32)
+        low = jnp.bitwise_and(cell_code, 31).astype(F32)
+        chigh = lax.dot_general((owner * high).astype(BF16), spot, nt, preferred_element_type=F32)
+        clow = lax.dot_general((owner * low).astype(BF16), spot, nt, preferred_element_type=F32)
+        cells = (chigh * 32.0 + clow).astype(jnp.int32) - 1
+        for k in range(4):
+            scell[4 * g + k] = cells[k:k + 1, :]
+            sbuf[g, k] = packed[CAP * k:CAP * k + CAP]
+        for k in range(4):
+            there = {"tile": z * 4 + k}
+            send(k != kme, sbuf.at[g, k], rbuf.at[g, kme], rec_recv.at[g], there)
+            send(k != kme, scell.at[4 * g + k], rcell.at[4 * g + kme], cell_recv.at[g], there)
+        rbuf[g, kme] = sbuf[g, kme]
+        rcell[4 * g + kme] = scell[4 * g + kme]
+
+    def share_list(g, data, meta):
+        share(g, data, jnp.right_shift(meta, 10), jnp.bitwise_and(meta, 1023))
+
     acc[...] = jnp.zeros_like(acc)
     dens[...] = jnp.zeros_like(dens)
     ones = jnp.ones((4 * CAP, 128), BF16)
@@ -161,22 +183,82 @@
         acc[rows, :] += jnp.dot(hit, rbuf[g].reshape(4 * CAP, 256), preferred_element_type=F32)
         dens[rows, :] += jnp.dot(hit, ones, preferred_element_type=F32)
 
-    def group(gd):
-        g = (NZ - gd) % NZ
-        if g == 0:
-            arrived(rbuf.at[0, pl.ds(0, 3)], rec_recv.at[0])
-        else:
-            arrived(rbuf.at[g], rec_recv.at[g])
-        return g, jnp.concatenate([rcell[4 * g + k] for k in range(4)], axis=1)
-
-    for gd in ORDER[:-1]:
-        g, ids = group(gd)
-
-        def step(r, _, g=g, ids=ids):
+    def group(g):
+        arrived(rcell.at[pl.ds(4 * g, 3)], cell_recv.at[g])
+        arrived(rbuf.at[g, pl.ds(0, 3)], rec_recv.at[g])
+        return jnp.concatenate([rcell[4 * g + k] for k in range(4)], axis=1)
+
+    def into_cells(g):
+        ids = group(g)
+
+        def step(r, _):
             chunk(g, ids, pl.multiple_of(r * 256, 256))
             return 0
 
         lax.fori_loop(0, 4, step, 0)
+
+    share(0, rec[...], slot, cell)
+
+    for way in range(2):
+        arrived(m1.at[way], meta_recv.at[way, 0])
+        send(None, m1.at[way], m2.at[way], meta_recv.at[way, 1], ahead[way])
+    for i in (3, 2, 1, 0):
+        rows = pl.ds(256 * i, 256)
+        for way in range(2):
+            arrived(h1.at[way, rows], ring_recv.at[way, i])
+            send(None, h1.at[way, rows], h2.at[way, rows], ring_recv.at[way, 4 + i], ahead[way])
+    for way in range(2):
+        share_list(1 + way, h1[way], m1[way])
+    into_cells(0)
+
+    for way in range(2):
+        arrived(m2.at[way], meta_recv.at[way, 1])
+        send(None, m2.at[way], m3.at[way], meta_recv.at[way, 2], ahead[way])
+    for i in (3, 2, 1, 0):
+        rows = pl.ds(256 * i, 256)
+        for way in range(2):
+            arrived(h2.at[way, rows], ring_recv.at[way, 4 + i])
+            if i > 0:
+                send(None, h2.at[way, rows], h3.at[way, pl.ds(256 * i - 256, 256)], ring_recv.at[way, 8 + i], ahead[way])
+    for way in range(2):
+        share_list(3 + way, h2[way], m2[way])
+    into_cells(1)
+    into_cells(2)
+
+    @pl.when(active)
+    def _():
+        wbuf[own_rows(dp), :] = wloc[...]
+        arrived(wbuf.at[pl.ds(0, 144 * (ndp // 2 - 1))], w_recv)
+
+    @pl.when(jnp.logical_not(active))
+    def _():
+        arrived(wbuf.at[pl.ds(0, 144 * (ndp // 2))], w_recv)
+
+    partner = at(x, y, z, 1 - c)
+    for i in range(ndp // 2):
+        rows = own_rows(2 * i + c)
+        send(None, wbuf.at[rows], wbuf.at[rows], f_recv, partner)
+
+    for way in range(2):
+        arrived(m3.at[way], meta_recv.at[way, 2])
+        send(None, m3.at[way], m4.at[way], meta_recv.at[way, 3], ahead[way])
+    for i in (3, 2, 1):
+        rows = pl.ds(256 * i - 256, 256)
+        for way in range(2):
+            arrived(h3.at[way, rows], ring_recv.at[way, 8 + i])
+            if i == 3:
+                send(None, h3.at[way, rows], h4.at[way], ring_recv.at[way, 8], ahead[way])
+    for way in range(2):
+        share_list(5 + way, h3[way], m3[way][:, 256:1024])
+    into_cells(3)
+    into_cells(4)
+    for way in range(2):
+        arrived(m4.at[way], meta_recv.at[way, 3])
+        arrived(h4.at[way], ring_recv.at[way, 8])
+    share_list(7, h4[...].reshape(512, 256),
+               jnp.concatenate([m4[0][:, 768:1024], m4[1][:, 768:1024]], axis=1))
+    into_cells(5)
+    into_cells(6)
 
     def spread(e):
         value = xbuf[e].astype(F32)
@@ -192,7 +274,8 @@
         value = acc[256 * r:256 * r + 256, :] * jnp.concatenate([inv, inv], axis=1)
         xbuf[r + 1] = value.astype(BF16)
 
-    g, ids = group(ORDER[-1])
+    g = 7
+    ids = group(g)
     chunk(g, ids, 0)
     finish(0)
     send(inner_top, xbuf.at[1], xbuf.at[5], h_recv.at[1], {"tile": tile - 1})
@@ -339,26 +422,22 @@
     @pl.when(both)
     def _():
         arrived(r4.at[pl.ds(0, 3)], recvs.at[12])
-        f5[z] = (r4[0] + r4[1]) + (r4[2] + r4[3])
-
-    for i in range(1, 8):
-        send(both, f5.at[z], f5.at[z], recvs.at[13], at(x, y, lax.rem(z + i, NZ), c))
+        f5[z] = ((r4[0] + r4[1]) + (r4[2] + r4[3])).astype(BF16)
+
+    for i in range(8):
+        zz = lax.rem(z + i, NZ)
+        for cc in ((1 - c,) if i == 0 else (c, 1 - c)):
+            send(both, f5.at[z], f5.at[z], recvs.at[13], at(x, y, zz, cc))
 
     @pl.when(both)
     def _():
         arrived(f5.at[pl.ds(0, 6)], recvs.at[13])
 
-    @pl.when(mine & (z == 7))
+    @pl.when(jnp.logical_not(both))
     def _():
         arrived(f5, recvs.at[13])
 
-    send(mine, f5, f5, recvs.at[14], partner)
-
-    @pl.when(jnp.logical_not(mine))
-    def _():
-        arrived(f5, recvs.at[14])
-
-    done = f5[...].reshape(448, 128)
+    done = f5[...].astype(F32).reshape(448, 128)
     for b in range(3):
         out_ref[:, 128 * b:128 * b + 128] = done[144 * b:144 * b + 144]
 
@@ -386,13 +465,15 @@
         out_specs=pl.BlockSpec(memory_space=pltpu.VMEM),
         scratch_shapes=[
             half(1024, 256), ints(1, 1024), ints(1, 1024), half(144, 384), half(1024, 384),
+            half(2, 1024, 256), ints(2, 1, 1024), half(2, 1024, 256), half(2, 1024, 256), half(2, 768, 256),
+            half(2, 256, 256), ints(2, 1, 1024), ints(2, 1, 1024), ints(2, 1, 1024), ints(2, 1, 1024),
             half(NZ, 4, CAP, 256), ints(NT, 1, CAP), half(NZ, 4, CAP, 256), ints(NT, 1, CAP),
             half(2304, 384), half(6, 256, 256), half(1536, 768), full(1024, 256), full(1024, 128),
             half(1024, 384), full(2304, 384),
             half(8, 144, 384), half(8, 144, 384), half(4, 448, 128), half(4, 448, 128),
             half(8, 448, 128), half(8, 4, 64, 128), full(448, 128), full(4, 64, 128),
-            full(8, 64, 128), full(8, 64, 128), full(2, 64, 128), full(4, 64, 128), full(7, 64, 128),
-            dma((5,)), dma((144,)), dma((NZ,)), dma, dma, dma, dma((2,)), dma((16,)),
+            full(8, 64, 128), full(8, 64, 128), full(2, 64, 128), full(4, 64, 128), half(7, 64, 128),
+            dma((5,)), dma((200,)), dma((2, 12)), dma((2, 4)), dma((NZ,)), dma((NZ,)), dma, dma, dma((2,)), dma((16,)),
         ],
         compiler_params=pltpu.CompilerParams(
             collective_id=0, has_side_effects=True, vmem_limit_bytes=58 * 1024 * 1024),

time: 129 us -> 106 us (0.82)
  Pallas kernels: 127 us -> 105 us
    pallas_call x1, Pallas kernels: 127 us -> 105 us  [local(): pl.pallas_call(fused, out_shape=jax.ShapeDtypeStruct((144, 384), F32), in...]
where the time goes in v3:
time: 106 us
  Pallas kernels  105 us (99%)
  local copies, waits for them, and re-layouts  1.64 us (2%)
    pallas_call x1, Pallas kernels, local(): pl.pallas_call(fused, out_shape=jax.ShapeDtypeStruct((144, 384), F32), in...  105 us

profile of v3, /device:TPU:1, one launch (start us, length us, event | category | flops | bytes accessed | tf_op | source)
XLA Modules:
  0.0 106.3 jit_solution(6515653760516499261)
XLA Ops:
  0.0 104.7 %shard_map.55 = f32[144,384]{1,0:T(8,128)} custom-call(bf16[1024,256]{1,0:T(8,128)(2,1)} %bitcast.4, s32[1,1024]{1,0:T(1,128)} %bitcast.5, s32[1,1024]{1,0:T(1,128)} %cell_hbm.1, bf16[144,384]{1,0:T(8,128)(2,1)} %w_hbm.1, bf16[1024,384]{1,0:T(8,128)(2,1)} %bitcast.3), custom_call_target="tpu_custom_call" | custom-call | tf_op jit(solution)/shard_map/pallas_call | solution.py:461
  104.7 1.6 %copy.7 = f32[144,384]{1,0:T(8,128)} copy(f32[144,384]{1,0:T(8,128)} %shard_map.55) | data formatting | bytes 442368

commit v4 on v3

--- a/solution.py
+++ b/solution.py
@@ -24,8 +24,8 @@
 def fused(rec_hbm, tile_hbm, cell_hbm, w_hbm, cot_hbm, out_ref,
           rec, til, cel, wloc, cot,
           lout, lmeta, h1, h2, h3, h4, m1, m2, m3, m4, sbuf, scell, rbuf, rcell, wbuf, xbuf, rmat, acc, dens, gp, grad,
-          s1, r1, s2a, s2b, ra2, rb2, pa3, pb3, ra3, rb3, q4, r4, f5,
-          local_sem, sends, ring_recv, meta_recv, rec_recv, cell_recv, w_recv, f_recv, h_recv, recvs):
+          s2, ra2, rb2, p3, r3, q4, r4, f5,
+          local_sem, sends, ring_recv, meta_recv, rec_recv, cell_recv, w_recv, f_recv, h_recv, x_recv, g_recv, recvs):
     tile = lax.axis_index("tile")
     dp = lax.axis_index("dp")
     z = lax.div(tile, 4)
@@ -260,164 +260,195 @@
     into_cells(5)
     into_cells(6)
 
+    def block(n, size=256, count=1):
+        return pl.ds(pl.multiple_of(n * size, size), size * count)
+
     def spread(e):
         value = xbuf[e].astype(F32)
-        rmat[pl.ds(e * 256, 256), 0:256] = pltpu.roll(value, 1, 0).astype(BF16)
-        rmat[pl.ds(e * 256, 256), 256:512] = value.astype(BF16)
-        rmat[pl.ds(e * 256, 256), 512:768] = pltpu.roll(value, 255, 0).astype(BF16)
-
-    first, last = tile == 0, tile == NT - 1
-    inner_top, inner_end = jnp.logical_not(first), jnp.logical_not(last)
+        rmat[block(e), 0:256] = pltpu.roll(value, 1, 0).astype(BF16)
+        rmat[block(e), 256:512] = value.astype(BF16)
+        rmat[block(e), 512:768] = pltpu.roll(value, 255, 0).astype(BF16)
+
+    rim = 9 * c
+    at_end = (tile == 0) | (tile == NT - 1)
+    inside = jnp.logical_not(at_end)
+    own = 4 * c
+    theirs = 4 - own
+    out_row, in_row = 3 * c, 3 - 3 * c
 
     def finish(r):
-        inv = 1.0 / (dens[256 * r:256 * r + 256, :] + 1.0)
-        value = acc[256 * r:256 * r + 256, :] * jnp.concatenate([inv, inv], axis=1)
-        xbuf[r + 1] = value.astype(BF16)
+        inv = 1.0 / (dens[block(r), :] + 1.0)
+        value = acc[block(r), :] * jnp.concatenate([inv, inv], axis=1)
+        xbuf[own + r + 1] = value.astype(BF16)
+
+    def hand_over(r):
+        e = own + r + 1
+        send(None, xbuf.at[e], xbuf.at[e], x_recv.at[r], partner)
 
     g = 7
     ids = group(g)
-    chunk(g, ids, 0)
-    finish(0)
-    send(inner_top, xbuf.at[1], xbuf.at[5], h_recv.at[1], {"tile": tile - 1})
-    chunk(g, ids, 768)
-    finish(3)
-    send(inner_end, xbuf.at[4], xbuf.at[0], h_recv.at[0], {"tile": tile + 1})
+    chunk(g, ids, pl.multiple_of(256 * out_row, 256))
+    finish(out_row)
+    send(inside, xbuf.at[own + out_row + 1], xbuf.at[9 - rim], h_recv, {"tile": tile - 1 + 2 * c})
+    chunk(g, ids, pl.multiple_of(256 * in_row, 256))
+    finish(in_row)
+    hand_over(in_row)
     chunk(g, ids, 256)
     chunk(g, ids, 512)
     finish(1)
     finish(2)
-    for e in range(1, 5):
-        spread(e)
+    hand_over(1)
+    hand_over(2)
+    hand_over(out_row)
+    for r in range(4):
+        spread(own + r + 1)
     arrived(wbuf.at[pl.ds(0, 144 * (ndp // 2))], f_recv)
     loads[4].wait()
 
     def conv(r, n):
         pre = jnp.zeros((256 * n, 384), F32)
         for p in range(3):
-            pre = pre + jnp.dot(rmat[256 * (r + p):256 * (r + p + n), :], wbuf[768 * p:768 * p + 768, :],
+            pre = pre + jnp.dot(rmat[block(own + r + p, count=n), :], wbuf[768 * p:768 * p + 768, :],
                                 preferred_element_type=F32)
         c0 = 0.7978845608028654
         sq = pre * pre
         th = jnp.tanh(c0 * pre * (1.0 + 0.044715 * sq))
         slope = 0.5 * (1.0 + th) + 0.5 * pre * (1.0 - th * th) * (c0 * (1.0 + 3.0 * 0.044715 * sq))
-        gp[256 * r:256 * (r + n), :] = (cot[256 * r:256 * (r + n), :].astype(F32) * slope).astype(BF16)
+        gp[block(own + r, count=n), :] = (cot[block(r, count=n), :].astype(F32) * slope).astype(BF16)
+
+    def hand_gp(r, n, which):
+        rows = block(own + r, count=n)
+        send(None, gp.at[rows], gp.at[rows], g_recv.at[which], partner)
+
+    def gp_arrived(n, which):
+        arrived(gp.at[pl.ds(0, 256 * n)], g_recv.at[which])
 
     tn = (((0,), (0,)), ((), ()))
 
-    def outer(r, n, p, q):
-        return lax.dot_general(
-            rmat[256 * (r + p):256 * (r + p + n), 256 * q:256 * q + 256], gp[256 * r:256 * (r + n), :],
-            tn, preferred_element_type=F32)
+    taps = ((0, 0, 1, 2), (0, 1, 2, 0), (0, 2, 2, 1), (1, 0, 2, 2))
+
+    def outer(row, n, fresh=False):
+        right = gp[block(row, count=n), :]
+
+        def put(rows, value):
+            if fresh:
+                grad[rows, :] = value
+            else:
+                grad[rows, :] += value
+
+        for i, (p0, q0, p1, q1) in enumerate(taps):
+            p = p0 + c * (p1 - p0)
+            q = q0 + c * (q1 - q0)
+            put(pl.ds(pl.multiple_of(256 * i + 128 * c, 128), 256), lax.dot_general(
+                rmat[block(row + p, count=n), block(q)], right, tn, preferred_element_type=F32))
+        put(pl.ds(pl.multiple_of(1024 - 1024 * c, 1024), 128), lax.dot_general(
+            rmat[block(row + 1, count=n), block(2 + c, 128)], right, tn, preferred_element_type=F32))
 
     conv(1, 2)
-    for p in range(3):
-        for q in range(3):
-            grad[256 * (3 * p + q):256 * (3 * p + q) + 256, :] = outer(1, 2, p, q)
-
-    @pl.when(first)
-    def _():
-        xbuf[0] = jnp.zeros((256, 256), BF16)
-
-    @pl.when(last)
-    def _():
-        xbuf[5] = jnp.zeros((256, 256), BF16)
-
-    @pl.when(inner_top)
-    def _():
-        arrived(xbuf.at[0], h_recv.at[0])
-
-    @pl.when(inner_end)
-    def _():
-        arrived(xbuf.at[5], h_recv.at[1])
-
-    spread(0)
-    spread(5)
-    conv(0, 1)
-    conv(3, 1)
-
-    for p in range(3):
-        for q in range(3):
-            grad[256 * (3 * p + q):256 * (3 * p + q) + 256, :] += outer(0, 1, p, q) + outer(3, 1, p, q)
-        for k in ((0, 1), (2, 3, 4), (5, 6, 7))[p]:
-            s1[k] = grad[own_rows(2 * k + 1 - c), :].astype(BF16)
-            send(None, s1.at[k], r1.at[k], recvs.at[k], partner)
+    hand_gp(1, 2, 0)
+    outer(own + 1, 2, fresh=True)
+    arrived(xbuf.at[0], x_recv.at[out_row])
+    spread(theirs + out_row + 1)
+    conv(in_row, 1)
+    hand_gp(in_row, 1, 1)
+    for r in (1, 2):
+        arrived(xbuf.at[0], x_recv.at[r])
+        spread(theirs + r + 1)
+    arrived(xbuf.at[0], x_recv.at[in_row])
+    spread(theirs + in_row + 1)
+    gp_arrived(2, 0)
+    outer(theirs + 1, 2)
+    gp_arrived(1, 1)
+    outer(jnp.int32(3), 2)
+
+    @pl.when(at_end)
+    def _():
+        xbuf[rim] = jnp.zeros((256, 256), BF16)
+
+    @pl.when(inside)
+    def _():
+        arrived(xbuf.at[rim], h_recv)
+
+    spread(rim)
+    conv(out_row, 1)
+    hand_gp(out_row, 1, 2)
+    outer(own + out_row, 1)
+    gp_arrived(1, 2)
+    outer(theirs + in_row, 1)
 
     def stacked(value):
         return jnp.concatenate([value[:, 128 * b:128 * b + 128] for b in range(3)], axis=0)
 
-    def paired(k):
-        arrived(r1.at[k], recvs.at[k])
-        return stacked(grad[own_rows(2 * k + c), :] + r1[k].astype(F32)).astype(BF16)
-
-    for jj in range(4):
-        j = 2 * jj + c
-        s2a[jj, 0:432] = paired(jj)
-        send(j != y, s2a.at[jj, pl.ds(0, 432)], ra2.at[y, pl.ds(0, 432)], recvs.at[8], at(x, j, z, c))
-
-        @pl.when(j == y)
-        def _(jj=jj):
-            ra2[y, 0:432] = s2a[jj, 0:432]
-
-    for jj in range(4):
-        s2b[jj, 0:432] = paired(4 + jj)
-        s2b[jj, 432:448] = jnp.zeros((16, 128), BF16)
+    core0, core1 = c == 0, c == 1
+
+    for j in range(8):
+        s2[j, 0:432] = stacked(grad[144 * j:144 * j + 144, :]).astype(BF16)
+        s2[j, 432:448] = jnp.zeros((16, 128), BF16)
+        send(core0 & (j != y), s2.at[j, pl.ds(0, 432)], ra2.at[y, pl.ds(0, 432)], recvs.at[8],
+             at(x, jnp.int32(j), z, c))
+
+        @pl.when(core0 & (j == y))
+        def _(j=j):
+            ra2[j, 0:432] = s2[j, 0:432]
+
     for j in range(7):
-        send(j != z, s2b.at[:, pl.ds(64 * j, 64)], rb2.at[z], recvs.at[9], at(x, y, j, c))
-
-        @pl.when(j == z)
+        send(core1 & (j != z), s2.at[:, pl.ds(64 * j, 64)], rb2.at[z], recvs.at[9], at(x, y, jnp.int32(j), c))
+
+        @pl.when(core1 & (j == z))
         def _(j=j):
-            rb2[j] = s2b[:, 64 * j:64 * j + 64]
-
-    mine = lax.rem(y + c, 2) == 0
+            rb2[j] = s2[:, 64 * j:64 * j + 64]
+
     low_z = z < 7
-    both = mine & low_z
-
-    @pl.when(mine)
+    both = (c == xhi) & low_z
+
+    @pl.when(core0)
     def _():
         arrived(ra2.at[pl.ds(0, 7), pl.ds(0, 432)], recvs.at[8])
         total = ra2[0, 0:432].astype(F32)
         for i in range(1, 8):
             total = total + ra2[i, 0:432].astype(F32)
-        pa3[0:432] = total
-        pa3[432:448] = jnp.zeros((16, 128), F32)
+        total = jnp.concatenate([total, jnp.zeros((16, 128), F32)], axis=0)
+        for j in range(7):
+            p3[j] = total[64 * j:64 * j + 64]
 
     for j in range(7):
-        send(mine & (j != z), pa3.at[pl.ds(64 * j, 64)], ra3.at[z], recvs.at[10], at(x, y, j, c))
-
-    @pl.when(low_z)
+        send(core0 & (j != z), p3.at[j], r3.at[z], recvs.at[10], at(x, y, jnp.int32(j), c))
+
+    @pl.when(core1 & low_z)
     def _():
         arrived(rb2.at[pl.ds(0, 7)], recvs.at[9])
         total = rb2[0].astype(F32)
         for i in range(1, 8):
             total = total + rb2[i].astype(F32)
-        pb3[...] = total
-
-    for jj in range(4):
-        j = 2 * jj + c
-        send(low_z & (j != y), pb3.at[jj], rb3.at[y], recvs.at[11], at(x, j, z, c))
-
-        @pl.when(low_z & (j == y))
-        def _(jj=jj):
-            rb3[y] = pb3[jj]
+        p3[...] = total
+
+    for j in range(8):
+        send(core1 & low_z & (j != y), p3.at[j], r3.at[y], recvs.at[11], at(x, jnp.int32(j), z, c))
+
+    @pl.when(core0 & low_z)
+    def _():
+        r3[z] = p3[z]
+        arrived(r3.at[pl.ds(0, 7)], recvs.at[10])
+
+    @pl.when(core1 & low_z)
+    def _():
+        r3[y] = p3[y]
+        arrived(r3.at[pl.ds(0, 7)], recvs.at[11])
+
+    @pl.when(low_z)
+    def _():
+        total = r3[0]
+        for i in range(1, 8):
+            total = total + r3[i]
+        q4[...] = total
+
+    for i in range(2):
+        xx = 2 * c + i
+        send(low_z & (xx != x), q4, r4.at[x], recvs.at[12], at(xx, y, z, c))
 
     @pl.when(both)
     def _():
-        ra3[z] = pa3[pl.ds(pl.multiple_of(64 * z, 64), 64)]
-        arrived(ra3.at[pl.ds(0, 7)], recvs.at[10])
-        total = ra3[0]
-        for i in range(1, 8):
-            total = total + ra3[i]
-        q4[0] = total
-        arrived(rb3.at[pl.ds(0, 7)], recvs.at[11])
-        total = rb3[0]
-        for i in range(1, 8):
-            total = total + rb3[i]
-        q4[1] = total
-        r4[x] = q4[xhi]
-
-    for i in range(1, 4):
-        xx = lax.rem(x + i, 4)
-        send(both, q4.at[lax.div(xx, 2)], r4.at[x], recvs.at[12], at(xx, y, z, c))
+        r4[x] = q4[...]
 
     @pl.when(both)
     def _():
@@ -468,12 +499,11 @@
             half(2, 1024, 256), ints(2, 1, 1024), half(2, 1024, 256), half(2, 1024, 256), half(2, 768, 256),
             half(2, 256, 256), ints(2, 1, 1024), ints(2, 1, 1024), ints(2, 1, 1024), ints(2, 1, 1024),
             half(NZ, 4, CAP, 256), ints(NT, 1, CAP), half(NZ, 4, CAP, 256), ints(NT, 1, CAP),
-            half(2304, 384), half(6, 256, 256), half(1536, 768), full(1024, 256), full(1024, 128),
-            half(1024, 384), full(2304, 384),
-            half(8, 144, 384), half(8, 144, 384), half(4, 448, 128), half(4, 448, 128),
-            half(8, 448, 128), half(8, 4, 64, 128), full(448, 128), full(4, 64, 128),
-            full(8, 64, 128), full(8, 64, 128), full(2, 64, 128), full(4, 64, 128), half(7, 64, 128),
-            dma((5,)), dma((200,)), dma((2, 12)), dma((2, 4)), dma((NZ,)), dma((NZ,)), dma, dma, dma((2,)), dma((16,)),
+            half(2304, 384), half(10, 256, 256), half(2560, 768), full(1024, 256), full(1024, 128),
+            half(2048, 384), full(1152, 384),
+            half(8, 448, 128), half(8, 448, 128), half(8, 8, 64, 128), full(8, 64, 128),
+            full(8, 64, 128), full(64, 128), full(4, 64, 128), half(7, 64, 128),
+            dma((5,)), dma((200,)), dma((2, 12)), dma((2, 4)), dma((NZ,)), dma((NZ,)), dma, dma, dma, dma((4,)), dma((3,)), dma((16,)),
         ],
         compiler_params=pltpu.CompilerParams(
             collective_id=0, has_side_effects=True, vmem_limit_bytes=58 * 1024 * 1024),

time: 106 us -> 104 us (0.981); the launches traced: 106 us -> 102 us
  Pallas kernels: 105 us -> 101 us
    pallas_call x1, Pallas kernels: 105 us -> 101 us  [local(): pl.pallas_call(fused, out_shape=jax.ShapeDtypeStruct((144, 384), F32), in...]
where the time goes in v4:
time: 104 us; the launch traced here: 102 us
  Pallas kernels  101 us (97%)
  local copies, waits for them, and re-layouts  1.64 us (2%)
    pallas_call x1, Pallas kernels, local(): pl.pallas_call(fused, out_shape=jax.ShapeDtypeStruct((144, 384), F32), in...  101 us

profile of v4, /device:TPU:1, one launch (start us, length us, event | category | flops | bytes accessed | tf_op | source)
XLA Modules:
  0.0 102.3 jit_solution(6193858662599967598)
XLA Ops:
  0.0 100.6 %shard_map.55 = f32[144,384]{1,0:T(8,128)} custom-call(bf16[1024,256]{1,0:T(8,128)(2,1)} %bitcast.4, s32[1,1024]{1,0:T(1,128)} %bitcast.5, s32[1,1024]{1,0:T(1,128)} %cell_hbm.1, bf16[144,384]{1,0:T(8,128)(2,1)} %w_hbm.1, bf16[1024,384]{1,0:T(8,128)(2,1)} %bitcast.3), custom_call_target="tpu_custom_call" | custom-call | tf_op jit(solution)/shard_map/pallas_call | solution.py:492
  100.7 1.6 %copy.7 = f32[144,384]{1,0:T(8,128)} copy(f32[144,384]{1,0:T(8,128)} %shard_map.55) | data formatting | bytes 442368

commit v5 on v4

--- a/solution.py
+++ b/solution.py
@@ -12,6 +12,7 @@
 NY = 8
 NT = 32
 CAP = 128
+FAR = (4, 3, 5, 2, 6, 1, 7)
 
 
 def remote(src, dst, send, recv, where):
@@ -61,6 +62,18 @@
         started.append((cond, copy))
         under(cond, lambda: copy().start())
 
+    loads = [pltpu.make_async_copy(a, b, local_sem.at[i]) for i, (a, b) in enumerate(
+        ((tile_hbm, til), (cell_hbm, cel), (rec_hbm, rec), (w_hbm, wloc), (cot_hbm, cot)))]
+    for load in loads:
+        load.start()
+
+    flushed = [0]
+
+    def flush(upto):
+        for cond, copy in started[flushed[0]:upto]:
+            under(cond, lambda copy=copy: copy().wait_send())
+        flushed[0] = upto
+
     barrier = pltpu.get_barrier_semaphore()
 
     def greet(where):
@@ -70,7 +83,7 @@
         greet({"dp": lax.rem(dp + i, ndp)})
         return 0
 
-    for i in (4, 3, 5, 2, 6, 1, 7):
+    for i in FAR:
         greet(at(x, y, lax.rem(z + i, NZ), c))
     for i in range(1, 8):
         greet(at(x, y, lax.rem(z + i, NZ), 1 - c))
@@ -80,10 +93,6 @@
     greet({"tile": lax.rem(tile + NT - 1, NT)})
     lax.fori_loop(1, ndp, greet_dp, 0)
     greet(at(3 - 2 * xhi - xlo, y, z, c))
-    loads = [pltpu.make_async_copy(a, b, local_sem.at[i]) for i, (a, b) in enumerate(
-        ((tile_hbm, til), (cell_hbm, cel), (rec_hbm, rec), (w_hbm, wloc), (cot_hbm, cot)))]
-    for load in loads:
-        load.start()
     loads[0].wait()
     loads[1].wait()
 
@@ -257,6 +266,7 @@
         arrived(h4.at[way], ring_recv.at[way, 8])
     share_list(7, h4[...].reshape(512, 256),
                jnp.concatenate([m4[0][:, 768:1024], m4[1][:, 768:1024]], axis=1))
+    flush(len(started) - 24)
     into_cells(5)
     into_cells(6)
 
@@ -381,49 +391,80 @@
 
     core0, core1 = c == 0, c == 1
 
-    for j in range(8):
-        s2[j, 0:432] = stacked(grad[144 * j:144 * j + 144, :]).astype(BF16)
-        s2[j, 432:448] = jnp.zeros((16, 128), BF16)
-        send(core0 & (j != y), s2.at[j, pl.ds(0, 432)], ra2.at[y, pl.ds(0, 432)], recvs.at[8],
-             at(x, jnp.int32(j), z, c))
-
-        @pl.when(core0 & (j == y))
-        def _(j=j):
-            ra2[j, 0:432] = s2[j, 0:432]
-
-    for j in range(7):
-        send(core1 & (j != z), s2.at[:, pl.ds(64 * j, 64)], rb2.at[z], recvs.at[9], at(x, y, jnp.int32(j), c))
-
-        @pl.when(core1 & (j == z))
-        def _(j=j):
-            rb2[j] = s2[:, 64 * j:64 * j + 64]
-
     low_z = z < 7
     both = (c == xhi) & low_z
+    before_sums = len(started)
+
+    def convert(j):
+        s2[j, 0:432] = stacked(grad[own_rows(j), :]).astype(BF16)
+        s2[j, 432:448] = jnp.zeros((16, 128), BF16)
+
+    halves = (pl.ds(0, 256), pl.ds(256, 176))
 
     @pl.when(core0)
     def _():
-        arrived(ra2.at[pl.ds(0, 7), pl.ds(0, 432)], recvs.at[8])
-        total = ra2[0, 0:432].astype(F32)
-        for i in range(1, 8):
-            total = total + ra2[i, 0:432].astype(F32)
-        total = jnp.concatenate([total, jnp.zeros((16, 128), F32)], axis=0)
-        for j in range(7):
-            p3[j] = total[64 * j:64 * j + 64]
-
-    for j in range(7):
-        send(core0 & (j != z), p3.at[j], r3.at[z], recvs.at[10], at(x, y, jnp.int32(j), c))
-
-    @pl.when(core1 & low_z)
-    def _():
-        arrived(rb2.at[pl.ds(0, 7)], recvs.at[9])
-        total = rb2[0].astype(F32)
-        for i in range(1, 8):
-            total = total + rb2[i].astype(F32)
-        p3[...] = total
-
-    for j in range(8):
-        send(core1 & low_z & (j != y), p3.at[j], r3.at[y], recvs.at[11], at(x, jnp.int32(j), z, c))
+        for i in FAR:
+            convert(lax.rem(y + i, NY))
+        convert(y)
+        ra2[y] = s2[y]
+
+    for h in range(2):
+        for i in FAR:
+            j = lax.rem(y + i, NY)
+            send(core0, s2.at[j, halves[h]], ra2.at[y, halves[h]], recvs.at[h], at(x, j, z, c))
+
+    for h in range(2):
+        fours = pl.ds(4 * h, 4)
+
+        @pl.when(core1)
+        def _(h=h, fours=fours):
+            for j in range(4 * h, 4 * h + 4):
+                convert(j)
+
+            @pl.when(low_z)
+            def _():
+                for j in range(4 * h, 4 * h + 4):
+                    rb2[z, j] = s2[j, block(z, 64)]
+
+        for i in FAR:
+            j = lax.rem(z + i, NZ)
+            send(core1 & (j < 7), s2.at[fours, block(j, 64)], rb2.at[z, fours], recvs.at[2 + h], at(x, y, j, c))
+
+    flush(before_sums)
+    before_second = len(started)
+    for h in range(2):
+        first_piece, pieces = 4 * h, 4 - h
+
+        @pl.when(core0)
+        def _(h=h, first_piece=first_piece, pieces=pieces):
+            arrived(ra2.at[pl.ds(0, 7), halves[h]], recvs.at[h])
+            n = 256 - 80 * h
+            total = ra2[0, 256 * h:256 * h + n].astype(F32)
+            for i in range(1, 8):
+                total = total + ra2[i, 256 * h:256 * h + n].astype(F32)
+            if h == 1:
+                total = jnp.concatenate([total, jnp.zeros((16, 128), F32)], axis=0)
+            for j in range(pieces):
+                p3[first_piece + j] = total[64 * j:64 * j + 64]
+
+        for i in FAR:
+            j = lax.rem(z + i, NZ)
+            send(core0 & (j >= first_piece) & (j < first_piece + pieces), p3.at[j], r3.at[z], recvs.at[10], at(x, y, j, c))
+
+        @pl.when(core1 & low_z)
+        def _(h=h):
+            arrived(rb2.at[pl.ds(0, 7), pl.ds(4 * h, 4)], recvs.at[2 + h])
+            for j in range(4 * h, 4 * h + 4):
+                total = rb2[0, j].astype(F32)
+                for i in range(1, 8):
+                    total = total + rb2[i, j].astype(F32)
+                p3[j] = total
+
+        for i in FAR:
+            j = lax.rem(y + i, NY)
+            send(core1 & low_z & (lax.div(j, 4) == h), p3.at[j], r3.at[y], recvs.at[11], at(x, j, z, c))
+
+    flush(before_second)
 
     @pl.when(core0 & low_z)
     def _():
@@ -446,6 +487,8 @@
         xx = 2 * c + i
         send(low_z & (xx != x), q4, r4.at[x], recvs.at[12], at(xx, y, z, c))
 
+    flush(len(started) - 2)
+
     @pl.when(both)
     def _():
         r4[x] = q4[...]
@@ -455,11 +498,13 @@
         arrived(r4.at[pl.ds(0, 3)], recvs.at[12])
         f5[z] = ((r4[0] + r4[1]) + (r4[2] + r4[3])).astype(BF16)
 
-    for i in range(8):
+    for i in FAR + (0,):
         zz = lax.rem(z + i, NZ)
         for cc in ((1 - c,) if i == 0 else (c, 1 - c)):
             send(both, f5.at[z], f5.at[z], recvs.at[13], at(x, y, zz, cc))
 
+    flush(len(started) - 15)
+
     @pl.when(both)
     def _():
         arrived(f5.at[pl.ds(0, 6)], recvs.at[13])
@@ -472,8 +517,7 @@
     for b in range(3):
         out_ref[:, 128 * b:128 * b + 128] = done[144 * b:144 * b + 144]
 
-    for cond, copy in started:
-        under(cond, lambda copy=copy: copy().wait_send())
+    flush(len(started))
 
 
 def local(records, obs_tile, obs_cell, conv_weight, cotangent):
@@ -503,7 +547,7 @@
             half(2048, 384), full(1152, 384),
             half(8, 448, 128), half(8, 448, 128), half(8, 8, 64, 128), full(8, 64, 128),
             full(8, 64, 128), full(64, 128), full(4, 64, 128), half(7, 64, 128),
-            dma((5,)), dma((200,)), dma((2, 12)), dma((2, 4)), dma((NZ,)), dma((NZ,)), dma, dma, dma, dma((4,)), dma((3,)), dma((16,)),
+            dma((5,)), dma((240,)), dma((2, 12)), dma((2, 4)), dma((NZ,)), dma((NZ,)), dma, dma, dma, dma((4,)), dma((3,)), dma((16,)),
         ],
         compiler_params=pltpu.CompilerParams(
             collective_id=0, has_side_effects=True, vmem_limit_bytes=58 * 1024 * 1024),

time: 104 us -> 105 us (level); the launches traced: 102 us -> 105 us
  Pallas kernels: 101 us -> 103 us
    pallas_call x1, Pallas kernels: 101 us -> 103 us  [local(): pl.pallas_call(fused, out_shape=jax.ShapeDtypeStruct((144, 384), F32), in...]
where the time goes in v5:
time: 105 us
  Pallas kernels  103 us (98%)
  local copies, waits for them, and re-layouts  1.64 us (2%)
    pallas_call x1, Pallas kernels, local(): pl.pallas_call(fused, out_shape=jax.ShapeDtypeStruct((144, 384), F32), in...  103 us

profile of v5, /device:TPU:1, one launch (start us, length us, event | category | flops | bytes accessed | tf_op | source)
XLA Modules:
  0.0 104.8 jit_solution(10641046571595523650)
XLA Ops:
  0.0 103.1 %shard_map.55 = f32[144,384]{1,0:T(8,128)} custom-call(bf16[1024,256]{1,0:T(8,128)(2,1)} %bitcast.4, s32[1,1024]{1,0:T(1,128)} %bitcast.5, s32[1,1024]{1,0:T(1,128)} %cell_hbm.1, bf16[144,384]{1,0:T(8,128)(2,1)} %w_hbm.1, bf16[1024,384]{1,0:T(8,128)(2,1)} %bitcast.3), custom_call_target="tpu_custom_call" | custom-call | tf_op jit(solution)/shard_map/pallas_call | solution.py:536
  103.2 1.6 %copy.7 = f32[144,384]{1,0:T(8,128)} copy(f32[144,384]{1,0:T(8,128)} %shard_map.55) | data formatting | bytes 442368

commit v6 on v5

--- a/solution.py
+++ b/solution.py
@@ -26,7 +26,7 @@
           rec, til, cel, wloc, cot,
           lout, lmeta, h1, h2, h3, h4, m1, m2, m3, m4, sbuf, scell, rbuf, rcell, wbuf, xbuf, rmat, acc, dens, gp, grad,
           s2, ra2, rb2, p3, r3, q4, r4, f5,
-          local_sem, sends, ring_recv, meta_recv, rec_recv, cell_recv, w_recv, f_recv, h_recv, x_recv, g_recv, recvs):
+          local_sem, news, sends, ring_recv, meta_recv, rec_recv, cell_recv, w_recv, f_recv, h_recv, x_recv, g_recv, recvs):
     tile = lax.axis_index("tile")
     dp = lax.axis_index("dp")
     z = lax.div(tile, 4)
@@ -79,20 +79,22 @@
     def greet(where):
         pl.semaphore_signal(barrier, inc=1, device_id=where, device_id_type=MESH)
 
-    def greet_dp(i, _):
-        greet({"dp": lax.rem(dp + i, ndp)})
-        return 0
-
-    for i in FAR:
-        greet(at(x, y, lax.rem(z + i, NZ), c))
-    for i in range(1, 8):
-        greet(at(x, y, lax.rem(z + i, NZ), 1 - c))
+    ahead = ({"tile": lax.rem(tile + 4, NT)}, {"tile": lax.rem(tile + NT - 4, NT)})
+    beside = (at(x, lax.rem(y + 1, NY), z, c), at(x, lax.rem(y + NY - 1, NY), z, c))
+    for where in ahead + beside:
+        greet(where)
     for k in range(1, 4):
         greet({"tile": z * 4 + lax.rem(kme + k, 4)})
-    greet({"tile": lax.rem(tile + 1, NT)})
-    greet({"tile": lax.rem(tile + NT - 1, NT)})
-    lax.fori_loop(1, ndp, greet_dp, 0)
-    greet(at(3 - 2 * xhi - xlo, y, z, c))
+    greet(at(lax.rem(x + 2, 4), y, z, c))
+    greet(at(3 - x, y, z, c))
+
+    def tell(n):
+        for where in ahead + beside:
+            pl.semaphore_signal(news.at[n], inc=1, device_id=where, device_id_type=MESH)
+
+    def hear(n):
+        pl.semaphore_wait(news.at[n], 4)
+
     loads[0].wait()
     loads[1].wait()
 
@@ -139,7 +141,6 @@
         return pl.ds(pl.multiple_of(144 * d, 16), 144)
 
     active = lax.rem(dp + c, 2) == 0
-    ahead = ({"tile": lax.rem(tile + 4, NT)}, {"tile": lax.rem(tile + NT - 4, NT)})
     for i in (3, 2, 1, 0):
         for way in range(2):
             rows = pl.ds(256 * i, 256)
@@ -149,13 +150,12 @@
             number = (got[0:1] * 64.0 + got[1:2]).astype(jnp.int32) - 1
             lmeta[way, :, rows] = number * 1024 + (got[2:3] * 32.0 + got[3:4]).astype(jnp.int32)
             if i == 3 and way == 0:
-                pl.semaphore_wait(barrier, 14 + 3 + 2 + ndp - 1 + 1)
+                pl.semaphore_wait(barrier, 9)
             send(None, lout.at[way, rows], h1.at[way, rows], ring_recv.at[way, i], ahead[way])
     for way in range(2):
         send(None, lmeta.at[way], m1.at[way], meta_recv.at[way, 0], ahead[way])
     loads[3].wait()
-    for i in range(1, ndp):
-        send(active, wloc, wbuf.at[own_rows(dp)], w_recv, {"dp": lax.rem(dp + i, ndp)})
+    tell(0)
     def share(g, data, number, cell_id):
         length = number.shape[1]
         rel = number - 512 * z
@@ -216,6 +216,11 @@
         for way in range(2):
             arrived(h1.at[way, rows], ring_recv.at[way, i])
             send(None, h1.at[way, rows], h2.at[way, rows], ring_recv.at[way, 4 + i], ahead[way])
+        hear(3 - i)
+        if i > 0:
+            tell(4 - i)
+    for i in range(1, ndp):
+        send(active, wloc, wbuf.at[own_rows(dp)], w_recv, {"dp": lax.rem(dp + i, ndp)})
     for way in range(2):
         share_list(1 + way, h1[way], m1[way])
     into_cells(0)
@@ -234,20 +239,6 @@
     into_cells(1)
     into_cells(2)
 
-    @pl.when(active)
-    def _():
-        wbuf[own_rows(dp), :] = wloc[...]
-        arrived(wbuf.at[pl.ds(0, 144 * (ndp // 2 - 1))], w_recv)
-
-    @pl.when(jnp.logical_not(active))
-    def _():
-        arrived(wbuf.at[pl.ds(0, 144 * (ndp // 2))], w_recv)
-
-    partner = at(x, y, z, 1 - c)
-    for i in range(ndp // 2):
-        rows = own_rows(2 * i + c)
-        send(None, wbuf.at[rows], wbuf.at[rows], f_recv, partner)
-
     for way in range(2):
         arrived(m3.at[way], meta_recv.at[way, 2])
         send(None, m3.at[way], m4.at[way], meta_recv.at[way, 3], ahead[way])
@@ -269,6 +260,21 @@
     flush(len(started) - 24)
     into_cells(5)
     into_cells(6)
+
+    @pl.when(active)
+    def _():
+        wbuf[own_rows(dp), :] = wloc[...]
+        arrived(wbuf.at[pl.ds(0, 144 * (ndp // 2 - 1))], w_recv)
+
+    @pl.when(jnp.logical_not(active))
+    def _():
+        arrived(wbuf.at[pl.ds(0, 144 * (ndp // 2))], w_recv)
+
+    partner = at(x, y, z, 1 - c)
+    for i in range(ndp // 2):
+        rows = own_rows(2 * i + c)
+        send(None, wbuf.at[rows], wbuf.at[rows], f_recv, partner)
+
 
     def block(n, size=256, count=1):
         return pl.ds(pl.multiple_of(n * size, size), size * count)
@@ -547,7 +553,7 @@
             half(2048, 384), full(1152, 384),
             half(8, 448, 128), half(8, 448, 128), half(8, 8, 64, 128), full(8, 64, 128),
             full(8, 64, 128), full(64, 128), full(4, 64, 128), half(7, 64, 128),
-            dma((5,)), dma((240,)), dma((2, 12)), dma((2, 4)), dma((NZ,)), dma((NZ,)), dma, dma, dma, dma((4,)), dma((3,)), dma((16,)),
+            dma((5,)), pltpu.SemaphoreType.REGULAR((4,)), dma((240,)), dma((2, 12)), dma((2, 4)), dma((NZ,)), dma((NZ,)), dma, dma, dma, dma((4,)), dma((3,)), dma((16,)),
         ],
         compiler_params=pltpu.CompilerParams(
             collective_id=0, has_side_effects=True, vmem_limit_bytes=58 * 1024 * 1024),

time: 105 us -> 107 us (1.019)
  Pallas kernels: 103 us -> 105 us
    pallas_call x1, Pallas kernels: 103 us -> 105 us  [local(): pl.pallas_call(fused, out_shape=jax.ShapeDtypeStruct((144, 384), F32), in...]
where the time goes in v6:
time: 107 us
  Pallas kernels  105 us (98%)
  local copies, waits for them, and re-layouts  1.64 us (2%)
    pallas_call x1, Pallas kernels, local(): pl.pallas_call(fused, out_shape=jax.ShapeDtypeStruct((144, 384), F32), in...  105 us

profile of v6, /device:TPU:1, one launch (start us, length us, event | category | flops | bytes accessed | tf_op | source)
XLA Modules:
  0.0 106.5 jit_solution(13315269185673788101)
XLA Ops:
  0.0 104.9 %shard_map.55 = f32[144,384]{1,0:T(8,128)} custom-call(bf16[1024,256]{1,0:T(8,128)(2,1)} %bitcast.4, s32[1,1024]{1,0:T(1,128)} %bitcast.5, s32[1,1024]{1,0:T(1,128)} %cell_hbm.1, bf16[144,384]{1,0:T(8,128)(2,1)} %w_hbm.1, bf16[1024,384]{1,0:T(8,128)(2,1)} %bitcast.3), custom_call_target="tpu_custom_call" | custom-call | tf_op jit(solution)/shard_map/pallas_call | solution.py:542
  104.9 1.6 %copy.7 = f32[144,384]{1,0:T(8,128)} copy(f32[144,384]{1,0:T(8,128)} %shard_map.55) | data formatting | bytes 442368

commit v7 on v6

--- a/solution.py
+++ b/solution.py
@@ -207,6 +207,10 @@
         lax.fori_loop(0, 4, step, 0)
 
     share(0, rec[...], slot, cell)
+    hear(0)
+    tell(1)
+    hear(1)
+    tell(2)
 
     for way in range(2):
         arrived(m1.at[way], meta_recv.at[way, 0])
@@ -216,11 +220,16 @@
         for way in range(2):
             arrived(h1.at[way, rows], ring_recv.at[way, i])
             send(None, h1.at[way, rows], h2.at[way, rows], ring_recv.at[way, 4 + i], ahead[way])
-        hear(3 - i)
-        if i > 0:
-            tell(4 - i)
-    for i in range(1, ndp):
-        send(active, wloc, wbuf.at[own_rows(dp)], w_recv, {"dp": lax.rem(dp + i, ndp)})
+        if i == 3:
+            hear(2)
+            tell(3)
+        if i == 2:
+            hear(3)
+            for n in FAR:
+                yy = lax.rem(y + n, NY)
+                send(active, wloc, wbuf.at[own_rows(dp)], w_recv, at(x, yy, z, c))
+                send(active, wloc, wbuf.at[own_rows(dp)], w_recv, at(3 - x, yy, z, c))
+            send(active, wloc, wbuf.at[own_rows(dp)], w_recv, at(3 - x, y, z, c))
     for way in range(2):
         share_list(1 + way, h1[way], m1[way])
     into_cells(0)

time: 107 us -> 102 us (0.953)
  Pallas kernels: 105 us -> 100 us
    pallas_call x1, Pallas kernels: 105 us -> 100 us  [local(): pl.pallas_call(fused, out_shape=jax.ShapeDtypeStruct((144, 384), F32), in...]
where the time goes in v7:
time: 102 us
  Pallas kernels  100 us (98%)
  local copies, waits for them, and re-layouts  1.64 us (2%)
    pallas_call x1, Pallas kernels, local(): pl.pallas_call(fused, out_shape=jax.ShapeDtypeStruct((144, 384), F32), in...  100 us

profile of v7, /device:TPU:1, one launch (start us, length us, event | category | flops | bytes accessed | tf_op | source)
XLA Modules:
  0.0 102.1 jit_solution(4146086367838675333)
XLA Ops:
  0.0 100.5 %shard_map.55 = f32[144,384]{1,0:T(8,128)} custom-call(bf16[1024,256]{1,0:T(8,128)(2,1)} %bitcast.4, s32[1,1024]{1,0:T(1,128)} %bitcast.5, s32[1,1024]{1,0:T(1,128)} %cell_hbm.1, bf16[144,384]{1,0:T(8,128)(2,1)} %w_hbm.1, bf16[1024,384]{1,0:T(8,128)(2,1)} %bitcast.3), custom_call_target="tpu_custom_call" | custom-call | tf_op jit(solution)/shard_map/pallas_call | solution.py:551
  100.5 1.6 %copy.7 = f32[144,384]{1,0:T(8,128)} copy(f32[144,384]{1,0:T(8,128)} %shard_map.55) | data formatting | bytes 442368

commit v8 on v7

--- a/solution.py
+++ b/solution.py
@@ -172,10 +172,12 @@
         for k in range(4):
             scell[4 * g + k] = cells[k:k + 1, :]
             sbuf[g, k] = packed[CAP * k:CAP * k + CAP]
-        for k in range(4):
+        turn = 1 - 2 * lax.rem(kme, 2)
+        across = lax.rem(kme + 2, 4)
+        for k in (across, across + turn, kme + turn):
             there = {"tile": z * 4 + k}
-            send(k != kme, sbuf.at[g, k], rbuf.at[g, kme], rec_recv.at[g], there)
-            send(k != kme, scell.at[4 * g + k], rcell.at[4 * g + kme], cell_recv.at[g], there)
+            send(None, sbuf.at[g, k], rbuf.at[g, kme], rec_recv.at[g], there)
+            send(None, scell.at[4 * g + k], rcell.at[4 * g + kme], cell_recv.at[g], there)
         rbuf[g, kme] = sbuf[g, kme]
         rcell[4 * g + kme] = scell[4 * g + kme]
 
@@ -212,9 +214,6 @@
     hear(1)
     tell(2)
 
-    for way in range(2):
-        arrived(m1.at[way], meta_recv.at[way, 0])
-        send(None, m1.at[way], m2.at[way], meta_recv.at[way, 1], ahead[way])
     for i in (3, 2, 1, 0):
         rows = pl.ds(256 * i, 256)
         for way in range(2):
@@ -231,12 +230,12 @@
                 send(active, wloc, wbuf.at[own_rows(dp)], w_recv, at(3 - x, yy, z, c))
             send(active, wloc, wbuf.at[own_rows(dp)], w_recv, at(3 - x, y, z, c))
     for way in range(2):
+        arrived(m1.at[way], meta_recv.at[way, 0])
+        send(None, m1.at[way], m2.at[way], meta_recv.at[way, 1], ahead[way])
+    for way in range(2):
         share_list(1 + way, h1[way], m1[way])
     into_cells(0)
 
-    for way in range(2):
-        arrived(m2.at[way], meta_recv.at[way, 1])
-        send(None, m2.at[way], m3.at[way], meta_recv.at[way, 2], ahead[way])
     for i in (3, 2, 1, 0):
         rows = pl.ds(256 * i, 256)
         for way in range(2):
@@ -244,13 +243,13 @@
             if i > 0:
                 send(None, h2.at[way, rows], h3.at[way, pl.ds(256 * i - 256, 256)], ring_recv.at[way, 8 + i], ahead[way])
     for way in range(2):
+        arrived(m2.at[way], meta_recv.at[way, 1])
+        send(None, m2.at[way], m3.at[way], meta_recv.at[way, 2], ahead[way])
+    for way in range(2):
         share_list(3 + way, h2[way], m2[way])
     into_cells(1)
     into_cells(2)
 
-    for way in range(2):
-        arrived(m3.at[way], meta_recv.at[way, 2])
-        send(None, m3.at[way], m4.at[way], meta_recv.at[way, 3], ahead[way])
     for i in (3, 2, 1):
         rows = pl.ds(256 * i - 256, 256)
         for way in range(2):
@@ -258,6 +257,9 @@
             if i == 3:
                 send(None, h3.at[way, rows], h4.at[way], ring_recv.at[way, 8], ahead[way])
     for way in range(2):
+        arrived(m3.at[way], meta_recv.at[way, 2])
+        send(None, m3.at[way], m4.at[way], meta_recv.at[way, 3], ahead[way])
+    for way in range(2):
         share_list(5 + way, h3[way], m3[way][:, 256:1024])
     into_cells(3)
     into_cells(4)
@@ -266,7 +268,7 @@
         arrived(h4.at[way], ring_recv.at[way, 8])
     share_list(7, h4[...].reshape(512, 256),
                jnp.concatenate([m4[0][:, 768:1024], m4[1][:, 768:1024]], axis=1))
-    flush(len(started) - 24)
+    flush(len(started) - 18)
     into_cells(5)
     into_cells(6)
 

time: 102 us -> 101 us (level)
    pallas_call x1, Pallas kernels: 100 us -> 99 us  [local(): pl.pallas_call(fused, out_shape=jax.ShapeDtypeStruct((144, 384), F32), in...]
where the time goes in v8:
time: 101 us
  Pallas kernels  99 us (98%)
  local copies, waits for them, and re-layouts  1.64 us (2%)
    pallas_call x1, Pallas kernels, local(): pl.pallas_call(fused, out_shape=jax.ShapeDtypeStruct((144, 384), F32), in...  99 us

profile of v8, /device:TPU:1, one launch (start us, length us, event | category | flops | bytes accessed | tf_op | source)
XLA Modules:
  0.0 100.7 jit_solution(7054465647034226008)
XLA Ops:
  0.0 99.0 %shard_map.55 = f32[144,384]{1,0:T(8,128)} custom-call(bf16[1024,256]{1,0:T(8,128)(2,1)} %bitcast.4, s32[1,1024]{1,0:T(1,128)} %bitcast.5, s32[1,1024]{1,0:T(1,128)} %cell_hbm.1, bf16[144,384]{1,0:T(8,128)(2,1)} %w_hbm.1, bf16[1024,384]{1,0:T(8,128)(2,1)} %bitcast.3), custom_call_target="tpu_custom_call" | custom-call | tf_op jit(solution)/shard_map/pallas_call | solution.py:553
  99.1 1.6 %copy.7 = f32[144,384]{1,0:T(8,128)} copy(f32[144,384]{1,0:T(8,128)} %shard_map.55) | data formatting | bytes 442368
